TPU v7x, 128 devices: a whole 4x4x4 slice. The times are simulated.
128 devices in a mesh: grp: 4 (over z_lo, core), wide: 32 (over y, x, z_hi).
Axes of the slice: x: 4, y: 4, z: 4 (z_hi: 2, z_lo: 2; z = z_hi * 2 + z_lo), core: 2. Of those that a mesh axis runs over, the one named last changes fastest.
Arguments:
- student_feats: bfloat16 [128, 256, 1280], P(('grp', 'wide')), may hold values from -6 to 6
- dino_in: bfloat16 [128, 256, 1536], P('grp', 'wide'), may hold values from -6 to 6
- siglip_in: bfloat16 [128, 256, 1152], P('grp', 'wide'), may hold values from -6 to 6
- sam_in: bfloat16 [128, 1024, 1280], P('grp', 'wide'), may hold values from -6 to 6
- dino_proj: bfloat16 [1536, 1536], P(None, 'wide'), may hold values from -0.15625 to 0.15625
- siglip_proj: bfloat16 [1152, 1152], P(None, 'wide'), may hold values from -0.1875 to 0.1875
- sam_proj: bfloat16 [1280, 1280], P(None, 'wide'), may hold values from -0.15625 to 0.15625
- dino_index: int32 [128, 256], P(('grp', 'wide')), may hold values from 0 to 255, as said below
- siglip_index: int32 [128, 256], P(('grp', 'wide')), may hold values from 0 to 255, as said below
- sam_index: int32 [128, 256], P(('grp', 'wide')), may hold values from 0 to 255, as said below
- dino_first: bfloat16 [1280, 640], P('wide'), may hold values from -0.15625 to 0.15625
- dino_second: bfloat16 [640, 1536], P('wide'), may hold values from -0.25 to 0.25
- siglip_first: bfloat16 [1280, 640], P('wide'), may hold values from -0.15625 to 0.15625
- siglip_second: bfloat16 [640, 1152], P('wide'), may hold values from -0.25 to 0.25
- sam_first: bfloat16 [1280, 640], P('wide'), may hold values from -0.15625 to 0.15625
- sam_second: bfloat16 [640, 1280], P('wide'), may hold values from -0.25 to 0.25
Outputs:
- dino_first_grad: float32 [1280, 640], P('wide')
- dino_second_grad: float32 [640, 1536], P('wide')
- siglip_first_grad: float32 [1280, 640], P('wide')
- siglip_second_grad: float32 [640, 1152], P('wide')
- sam_first_grad: float32 [1280, 640], P('wide')
- sam_second_grad: float32 [640, 1280], P('wide')
Inputs may be any that keep to these rules, and one draw needn't show every extreme that they name: dino_index[i, s] is the cell of the 16 x 16 grid under student patch s of image i, after that image's optional left-right mirror. siglip_index[i, s] is the cell of the 16 x 16 grid under student patch s of image i, after that image's optional left-right mirror. sam_index[i, s] is the block of the 16 x 16 grid of SAM blocks under student patch s of image i, after that image's optional left-right mirror.
All inputs are finite; a program needn't handle non-finite values.
Results may differ from a plain program's by a relative error of at most 0.002.
Values may be sent and summed in bfloat16 or wider, within the bound.
A program may use at most 128 MiB of HBM per device.

v0:
```python
import math

import jax
import jax.numpy as jnp
from jax import lax
from jax.sharding import PartitionSpec as P

SIDE = 16
GRID_M = 32


def layer_norm(values):
    centered = values - jnp.mean(values, axis=-1, keepdims=True)
    variance = jnp.mean(centered * centered, axis=-1, keepdims=True)
    return centered * lax.rsqrt(variance + 1e-05)


def gelu_pair(act):
    cdf = 0.5 * (1.0 + jax.scipy.special.erf(act * (1.0 / math.sqrt(2.0))))
    density = jnp.exp(-0.5 * act * act) * (1.0 / math.sqrt(2.0 * math.pi))
    return (act * cdf, cdf + act * density)


def take_cells(cell_map, cell_index):
    return cell_map[cell_index]


def pick_rows(maps, index):
    chosen = jax.vmap(take_cells)(maps, index)
    return chosen.reshape(-1, chosen.shape[-1])


def teacher_layer(rows, projection):
    whole = lax.all_gather(projection, "wide", axis=1, tiled=True)
    mixed = jnp.dot(rows, whole, preferred_element_type=jnp.float32)
    return layer_norm(rows.astype(jnp.float32) + mixed).astype(jnp.bfloat16)


def source_maps(inputs, projection):
    images, cells, width = inputs.shape
    return teacher_layer(inputs.reshape(images * cells, width), projection).reshape(
        images, cells, width
    )


def pool_blocks(maps):
    ratio = GRID_M // SIDE
    group_cells = ratio * ratio
    images, cells, width = maps.shape
    held = lax.optimization_barrier(maps)
    blocks = held.astype(jnp.float32).reshape(images, cells // group_cells, group_cells, width)
    return jnp.mean(blocks, axis=2).astype(jnp.bfloat16)


def adaptor_grads(normed, target, first, second, factor):
    act = jnp.dot(
        normed,
        lax.all_gather(first, "wide", axis=0, tiled=True),
        preferred_element_type=jnp.float32,
    )
    hid_full, slope = gelu_pair(act)
    hidden = hid_full.astype(jnp.bfloat16)
    whole_second = lax.all_gather(second, "wide", axis=0, tiled=True)
    pred = jnp.dot(hidden, whole_second, preferred_element_type=jnp.float32)
    grad_pred = (factor * (pred - target.astype(jnp.float32))).astype(jnp.bfloat16)
    grad_hid = lax.dot_general(
        grad_pred, whole_second, (((1,), (1,)), ((), ())), preferred_element_type=jnp.float32
    )
    grad_act = (grad_hid * slope).astype(jnp.bfloat16)
    first_part = lax.dot_general(
        normed, grad_act, (((0,), (0,)), ((), ())), preferred_element_type=jnp.float32
    )
    second_part = lax.dot_general(
        hidden, grad_pred, (((0,), (0,)), ((), ())), preferred_element_type=jnp.float32
    )
    return (first_part, second_part)


def body(
    student_feats,
    dino_in,
    siglip_in,
    sam_in,
    dino_proj,
    siglip_proj,
    sam_proj,
    dino_index,
    siglip_index,
    sam_index,
    dino_first,
    dino_second,
    siglip_first,
    siglip_second,
    sam_first,
    sam_second,
):
    group_count = lax.axis_size("grp")
    wide_count = lax.axis_size("wide")
    images_total = student_feats.shape[0] * group_count * wide_count
    dino_maps, siglip_maps, sam_maps = (
        lax.all_to_all(
            source_maps(dino_in, dino_proj), "wide", split_axis=0, concat_axis=1, tiled=True
        ),
        lax.all_to_all(
            source_maps(siglip_in, siglip_proj), "wide", split_axis=0, concat_axis=1, tiled=True
        ),
        lax.all_to_all(
            pool_blocks(source_maps(sam_in, sam_proj)),
            "wide",
            split_axis=0,
            concat_axis=1,
            tiled=True,
        ),
    )
    dino_target = pick_rows(dino_maps, dino_index)
    siglip_target = pick_rows(siglip_maps, siglip_index)
    sam_target = pick_rows(sam_maps, sam_index)
    width = student_feats.shape[-1]
    normed = layer_norm(student_feats.reshape(-1, width).astype(jnp.float32)).astype(jnp.bfloat16)
    factor = 2.0 / images_total
    dino_one, dino_two = adaptor_grads(normed, dino_target, dino_first, dino_second, factor)
    siglip_one, siglip_two = adaptor_grads(
        normed, siglip_target, siglip_first, siglip_second, factor
    )
    sam_one, sam_two = adaptor_grads(normed, sam_target, sam_first, sam_second, factor)
    shards = (
        lax.psum_scatter(dino_one, "wide", scatter_dimension=0, tiled=True),
        lax.psum_scatter(dino_two, "wide", scatter_dimension=0, tiled=True),
        lax.psum_scatter(siglip_one, "wide", scatter_dimension=0, tiled=True),
        lax.psum_scatter(siglip_two, "wide", scatter_dimension=0, tiled=True),
        lax.psum_scatter(sam_one, "wide", scatter_dimension=0, tiled=True),
        lax.psum_scatter(sam_two, "wide", scatter_dimension=0, tiled=True),
    )
    results = lax.psum((shards[0], shards[1], shards[2], shards[3], shards[4], shards[5]), "grp")
    return (results[0], results[1], results[2], results[3], results[4], results[5])


def solution(mesh):
    placed = (
        P(("grp", "wide"), None, None),
        P("grp", "wide", None),
        P("grp", "wide", None),
        P("grp", "wide", None),
        P(None, "wide"),
        P(None, "wide"),
        P(None, "wide"),
        P(("grp", "wide"), None),
        P(("grp", "wide"), None),
        P(("grp", "wide"), None),
        P("wide", None),
        P("wide", None),
        P("wide", None),
        P("wide", None),
        P("wide", None),
        P("wide", None),
    )
    return jax.shard_map(
        body,
        mesh=mesh,
        in_specs=placed,
        out_specs=(
            P("wide", None),
            P("wide", None),
            P("wide", None),
            P("wide", None),
            P("wide", None),
            P("wide", None),
        ),
        check_vma=False,
    )
```

profile of v0, /device:TPU:1, one launch (start us, length us, event | category | flops | bytes accessed | tf_op | source)
XLA Modules:
  0.0 1707.5 jit_solution(752453932026787211)
XLA Ops:
  13.4 1.3 convert_reduce_fusion
  15.0 73.9 %all-gather.28.cloned.1.call-done = bf16[32,36,1152]{2,1,0:T(8,128)(2,1)} async-done(((bf16[1,36,1152]{2,1,0:T(8,128)(2,1)}), bf16[32,36,1152]{2,1,0:T(8,128)(2,1)}) %all-gather.28.cloned.1.call-update) | async-done | bytes 2654224 | tf_op jit(solution)/shard_map/all_gather | solution.py:34
  89.0 5.2 reshape.152
  94.1 2.9 fusion.78
  98.3 4.1 all-to-all-start.1
  102.5 57.4 %all-gather.26.cloned.1.call-done = bf16[32,20,1152]{2,1,0:T(8,128)(2,1)} async-done(((bf16[1,20,1152]{2,1,0:T(8,128)(2,1)}), bf16[32,20,1152]{2,1,0:T(8,128)(2,1)}) %all-gather.26.cloned.1.call-update) | async-done | bytes 1474576 | tf_op jit(solution)/shard_map/all_gather | solution.py:63
  159.9 2.3 reshape.150
  162.3 67.3 %all-gather.18.cloned.1.call-done = bf16[1280,640]{1,0:T(8,128)(2,1)} async-done(((bf16[40,640]{1,0:T(8,128)(2,1)}), bf16[1280,640]{1,0:T(8,128)(2,1)}) %all-gather.18.cloned.1.call-update) | async-done | bytes 1638416 | tf_op jit(solution)/shard_map/all_gather | solution.py:58
  229.5 3.0 fusion.69
  232.6 3.5 gather_fusion.1
  236.1 2.0 fusion.6
  238.1 2.3 fusion.64
  240.7 3.1 fusion.17
  244.5 62.9 %all-gather.22.cloned.1.call-done = bf16[1280,1280]{0,1:T(8,128)(2,1)} async-done(((bf16[1280,40]{0,1:T(8,128)(2,1)}), bf16[1280,1280]{0,1:T(8,128)(2,1)}) %all-gather.22.cloned.1.call-update) | async-done | bytes 3276816 | tf_op jit(solution)/shard_map/all_gather | solution.py:34
  307.3 7.2 fusion.77
  315.2 2.1 multiply_convert_fusion
  317.3 6.1 reshape.115
  323.3 5.8 reduce_sum.89
  330.1 4.2 all-to-all-start.2
  334.5 47.3 %all-gather.30.cloned.1.call-done = bf16[32,20,1280]{2,1,0:T(8,128)(2,1)} async-done(((bf16[1,20,1280]{2,1,0:T(8,128)(2,1)}), bf16[32,20,1280]{2,1,0:T(8,128)(2,1)}) %all-gather.30.cloned.1.call-update) | async-done | bytes 1638416 | tf_op jit(solution)/shard_map/all_gather | solution.py:63
  381.9 2.5 reshape.154
  384.3 66.7 %all-gather.20.cloned.1.call-done = bf16[1280,640]{1,0:T(8,128)(2,1)} async-done(((bf16[40,640]{1,0:T(8,128)(2,1)}), bf16[1280,640]{1,0:T(8,128)(2,1)}) %all-gather.20.cloned.1.call-update) | async-done | bytes 1638416 | tf_op jit(solution)/shard_map/all_gather | solution.py:58
  451.0 3.0 fusion.66
  454.1 3.7 gather_fusion.2
  457.8 2.9 fusion.7
  460.7 4.2 fusion.18
  464.9 71.2 %all-gather.16.cloned.1.call-done = bf16[1536,1536]{0,1:T(8,128)(2,1)} async-done(((bf16[1536,48]{0,1:T(8,128)(2,1)}), bf16[1536,1536]{0,1:T(8,128)(2,1)}) %all-gather.16.cloned.1.call-update) | async-done | bytes 4718608 | tf_op jit(solution)/shard_map/all_gather | solution.py:34
  536.2 3.8 fusion.76
  541.5 4.9 all-to-all-start
  546.7 64.1 %all-gather.14.cloned.1.call-done = bf16[1280,640]{1,0:T(8,128)(2,1)} async-done(((bf16[40,640]{1,0:T(8,128)(2,1)}), bf16[1280,640]{1,0:T(8,128)(2,1)}) %all-gather.14.cloned.1.call-update) | async-done | bytes 1638416 | tf_op jit(solution)/shard_map/all_gather | solution.py:58
  610.9 3.0 fusion.72
  613.9 70.2 %all-gather.24.cloned.1.call-done = bf16[32,20,1536]{2,1,0:T(8,128)(2,1)} async-done(((bf16[1,20,1536]{2,1,0:T(8,128)(2,1)}), bf16[32,20,1536]{2,1,0:T(8,128)(2,1)}) %all-gather.24.cloned.1.call-update) | async-done | bytes 1966096 | tf_op jit(solution)/shard_map/all_gather | solution.py:63
  684.1 2.6 reshape.148
  686.7 4.2 gather_fusion
  690.8 3.1 fusion.5
  694.0 4.5 fusion.16
  698.6 2.1 fusion.63
  700.6 2.6 fusion.62
  703.2 272.5 %fusion.74 = (f32[24,1536]{1,0:T(8,128)S(1)}, f32[24,1280]{1,0:T(8,128)S(1)}) fusion(f32[640,1536]{1,0:T(8,128)} %fusion.62, f32[640,1280]{1,0:T(8,128)S(1)} %fusion.63), kind=kCustom, calls=%all-reduce-scatter.2 | all-reduce-scatter fusion | flops 2162689 | bytes 7479808
  975.8 1.3 collective-permute-start.10
  977.1 6.2 collective-permute-start.11
  985.2 1.3 collective-permute-start.6
  986.5 3.8 collective-permute-start.7
  990.3 5.7 collective-permute-start.8
  996.0 4.8 collective-permute-start.9
  1000.8 1.9 collective-permute-start.5
  1002.7 65.8 %all-reduce.13.cloned.1.call-done = f32[640,1152]{1,0:T(8,128)} async-done(((f32[640,1152]{1,0:T(8,128)}), f32[640,1152]{1,0:T(8,128)}) %all-reduce.13.cloned.1.call-update) | async-done | bytes 2949136
  1068.6 1.6 constant_dynamic-slice_fusion.2
  1070.1 1.5 collective-permute-start
  1071.7 2.2 collective-permute-start.1
  1073.9 1.6 collective-permute-start.2
  1075.6 1.3 collective-permute-start.3
  1077.9 2.4 collective-permute-start.4
  1081.0 1.4 collective-permute-done.4
  1084.1 169.3 %reduce-scatter.19.cloned.1.call-done = f32[40,640]{1,0:T(8,128)} async-done(((f32[1280,640]{1,0:T(8,128)}), f32[40,640]{1,0:T(8,128)}) %reduce-scatter.19.cloned.1.call-update) | async-done | bytes 102416
  1253.4 189.2 %reduce-scatter.21.cloned.1.call-done = f32[40,640]{1,0:T(8,128)} async-done(((f32[1280,640]{1,0:T(8,128)}), f32[40,640]{1,0:T(8,128)}) %reduce-scatter.21.cloned.1.call-update) | async-done | bytes 102416
  1442.6 188.3 %reduce-scatter.17.cloned.1.call-done = f32[40,640]{1,0:T(8,128)} async-done(((f32[1280,640]{1,0:T(8,128)}), f32[40,640]{1,0:T(8,128)}) %reduce-scatter.17.cloned.1.call-update) | async-done | bytes 102416
  1630.9 60.7 %all-reduce.15.cloned.1.call-done = (f32[40,640]{1,0:T(8,128)}, f32[20,1536]{1,0:T(8,128)}, f32[40,640]{1,0:T(8,128)}, f32[20,1152]{1,0:T(8,128)}, f32[40,640]{1,0:T(8,128)}, /*index=5*/f32[20,1280]{1,0:T(8,128)}) async-done(((f32[40,640]{1,0:T(8,128)}, f32[20,1536]{1,0:T(8,128)}, f32[40,640]{1,0:T(8,128)}, f32[20,1152]{1,0:T(8,128)}, f32[40,640]{1,0:T(8,128)}, /*index=5*/f32[20,1280]{1,0:T(8,128)}), ...) | async-done | bytes 624656 | tf_op jit(solution)/shard_map/psum | solution.py:134
  1691.6 1.5 copy.29
  1693.2 1.6 copy.30
  1694.8 1.5 copy.31
  1696.3 1.5 copy.32
  1697.8 1.5 copy.33
  1699.4 1.6 copy.34
  (97 shorter events, 16.5 us)
Async XLA Ops:
  7.2 7.5 copy-start
  7.2 7.8 copy-start.7
  7.2 81.8 %all-gather.28.cloned.1.call-start = ((), (), s32[]{:S(2)}) async-start(), calls=%async_computation.13 | async-start | bytes 3041280 | tf_op jit(solution)/shard_map/all_gather | solution.py:34
  7.9 152.0 %all-gather.26.cloned.1.call-start = ((), (), s32[]{:S(2)}) async-start(), calls=%async_computation.12 | async-start | bytes 1824768 | tf_op jit(solution)/shard_map/all_gather | solution.py:63
  8.7 220.8 %all-gather.18.cloned.1.call-start = ((), (), s32[]{:S(2)}) async-start(), calls=%async_computation.8 | async-start | bytes 1689600 | tf_op jit(solution)/shard_map/all_gather | solution.py:58
  9.4 297.9 %all-gather.22.cloned.1.call-start = ((), (), s32[]{:S(2)}) async-start(), calls=%async_computation.10 | async-start | bytes 3379200 | tf_op jit(solution)/shard_map/all_gather | solution.py:34
  10.0 371.9 %all-gather.30.cloned.1.call-start = ((), (), s32[]{:S(2)}) async-start(), calls=%async_computation.14 | async-start | bytes 2027520 | tf_op jit(solution)/shard_map/all_gather | solution.py:63
  10.6 440.5 %all-gather.20.cloned.1.call-start = ((), (), s32[]{:S(2)}) async-start(), calls=%async_computation.9 | async-start | bytes 1689600 | tf_op jit(solution)/shard_map/all_gather | solution.py:58
  11.1 525.0 %all-gather.16.cloned.1.call-start = ((), (), s32[]{:S(2)}) async-start(), calls=%async_computation.7 | async-start | bytes 4866048 | tf_op jit(solution)/shard_map/all_gather | solution.py:34
  11.9 599.0 %all-gather.14.cloned.1.call-start = ((), (), s32[]{:S(2)}) async-start(), calls=%async_computation.6 | async-start | bytes 1689600 | tf_op jit(solution)/shard_map/all_gather | solution.py:58
  12.6 671.5 %all-gather.24.cloned.1.call-start = ((), (), s32[]{:S(2)}) async-start(), calls=%async_computation.11 | async-start | bytes 2433024 | tf_op jit(solution)/shard_map/all_gather | solution.py:63
  15.0 79.1 %copy-start.11 = (bf16[32,8,1152]{2,1,0:T(8,128)(2,1)S(1)}, bf16[32,8,1152]{2,1,0:T(8,128)(2,1)}, u32[]{:S(2)}) copy-start(bf16[32,8,1152]{2,1,0:T(8,128)(2,1)} %param.18) | copy-start | bytes 1769476
  98.3 134.2 %all-to-all-start.1 = ((bf16[32,8,1152]{2,1,0:T(8,128)(2,1)}), bf16[32,8,1152]{2,1,0:T(8,128)(2,1)S(1)}, u32[]{:S(2)}, u32[]{:S(2)}) async-start(bf16[32,8,1152]{2,1,0:T(8,128)(2,1)} %fusion.36), calls=%async_computation.1 | async-start | bytes 1179648 | tf_op jit(solution)/shard_map/all_to_all | solution.py:104
  102.5 966.1 %all-reduce.13.cloned.1.call-start = ((), (), s32[]{:S(2)}) async-start(), calls=%async_computation.15 | async-start | bytes 5898240
  236.1 2.0 copy-start.5
  240.4 1013.0 %reduce-scatter.19.cloned.1.call-start = ((), (), s32[]{:S(2)}) async-start(), calls=%async_computation.17 | async-start | bytes 3379200
  243.8 0.7 copy-start.8
  330.1 124.0 %all-to-all-start.2 = ((bf16[32,8,1280]{2,1,0:T(8,128)(2,1)}), bf16[32,8,1280]{2,1,0:T(8,128)(2,1)S(1)}, u32[]{:S(2)}, u32[]{:S(2)}) async-start(bf16[32,8,1280]{2,1,0:T(8,128)(2,1)} %multiply_convert_fusion.2), calls=%async_computation.2 | async-start | bytes 1310720 | tf_op jit(solution)/shard_map/all_to_all | solution.py:107
  334.3 1108.3 %reduce-scatter.21.cloned.1.call-start = ((), (), s32[]{:S(2)}) async-start(), calls=%async_computation.18 | async-start | bytes 3379200
  457.8 2.9 copy-start.4
  464.9 71.2 %copy-start.10 = (bf16[32,8,1536]{2,1,0:T(8,128)(2,1)S(1)}, bf16[32,8,1536]{2,1,0:T(8,128)(2,1)}, u32[]{:S(2)}) copy-start(bf16[32,8,1536]{2,1,0:T(8,128)(2,1)} %param.17) | copy-start | bytes 2359300
  540.3 6.4 copy-start.9
  541.5 145.2 %all-to-all-start = ((bf16[32,8,1536]{2,1,0:T(8,128)(2,1)}), bf16[32,8,1536]{2,1,0:T(8,128)(2,1)S(1)}, u32[]{:S(2)}, u32[]{:S(2)}) async-start(bf16[32,8,1536]{2,1,0:T(8,128)(2,1)} %fusion.19), calls=%async_computation | async-start | bytes 1572864 | tf_op jit(solution)/shard_map/all_to_all | solution.py:101
  546.4 1084.5 %reduce-scatter.17.cloned.1.call-start = ((), (), s32[]{:S(2)}) async-start(), calls=%async_computation.16 | async-start | bytes 3379200
  690.8 3.1 copy-start.1
  698.5 993.1 %all-reduce.15.cloned.1.call-start = ((), (), s32[]{:S(2)}) async-start(), calls=%async_computation.19 | async-start | bytes 1376256 | tf_op jit(solution)/shard_map/psum | solution.py:134
  698.5 2.1 copy-start.2
  698.6 2.1 copy-start.3
  703.2 280.0 %copy-start.6 = (u32[128]{0:T(128)S(1)}, u32[128]{0:T(128)}, u32[]{:S(2)}) copy-start(u32[128]{0:T(128)} %constant.100) | copy-start | bytes 1540
  975.8 25.0 %collective-permute-start.10 = (f32[24,1280]{1,0:T(8,128)S(1)}, f32[24,1280]{1,0:T(8,128)S(1)}, u32[]{:S(2)}, u32[]{:S(2)}) collective-permute-start(f32[24,1280]{1,0:T(8,128)S(1)} %get-tuple-element.15), channel_id=1, source_target_pairs={{0,5},{1,6},{2,7},{3,8},{4,9},{5,10},{6,11},{7,12},{8,13},{9,14},{... | collective-permute-start | bytes 368648
  977.1 18.9 %collective-permute-start.11 = (f32[4,1280]{1,0:T(4,128)S(1)}, f32[4,1280]{1,0:T(4,128)S(1)}, u32[]{:S(2)}, u32[]{:S(2)}) collective-permute-start(f32[4,1280]{1,0:T(4,128)S(1)} %slice.13), channel_id=1, source_target_pairs={{0,6},{1,7},{2,8},{3,9},{4,10},{5,11},{6,12},{7,13},{8,14},{9,15},... | collective-permute-start | bytes 61448
  985.2 84.9 %collective-permute-start.6 = (f32[24,1280]{1,0:T(8,128)S(1)}, f32[24,1280]{1,0:T(8,128)S(1)}, u32[]{:S(2)}, u32[]{:S(2)}) collective-permute-start(f32[24,1280]{1,0:T(8,128)S(1)} %get-tuple-element.15), channel_id=1, source_target_pairs={{0,1},{1,2},{2,3},{3,4},{4,5},{5,6},{6,7},{7,8},{8,9},{9,10},{10,1... | collective-permute-start | bytes 368648
  986.5 85.2 %collective-permute-start.7 = (f32[24,1280]{1,0:T(8,128)S(1)}, f32[24,1280]{1,0:T(8,128)S(1)}, u32[]{:S(2)}, u32[]{:S(2)}) collective-permute-start(f32[24,1280]{1,0:T(8,128)S(1)} %get-tuple-element.15), channel_id=1, source_target_pairs={{0,2},{1,3},{2,4},{3,5},{4,6},{5,7},{6,8},{7,9},{8,10},{9,11},{10,... | collective-permute-start | bytes 368648
  990.3 83.6 %collective-permute-start.8 = (f32[24,1280]{1,0:T(8,128)S(1)}, f32[24,1280]{1,0:T(8,128)S(1)}, u32[]{:S(2)}, u32[]{:S(2)}) collective-permute-start(f32[24,1280]{1,0:T(8,128)S(1)} %get-tuple-element.15), channel_id=1, source_target_pairs={{0,3},{1,4},{2,5},{3,6},{4,7},{5,8},{6,9},{7,10},{8,11},{9,12},{10... | collective-permute-start | bytes 368648
  996.0 79.5 %collective-permute-start.9 = (f32[24,1280]{1,0:T(8,128)S(1)}, f32[24,1280]{1,0:T(8,128)S(1)}, u32[]{:S(2)}, u32[]{:S(2)}) collective-permute-start(f32[24,1280]{1,0:T(8,128)S(1)} %get-tuple-element.15), channel_id=1, source_target_pairs={{0,4},{1,5},{2,6},{3,7},{4,8},{5,9},{6,10},{7,11},{8,12},{9,13},{1... | collective-permute-start | bytes 368648
  1000.8 77.1 %collective-permute-start.5 = (f32[4,1536]{1,0:T(4,128)S(1)}, f32[4,1536]{1,0:T(4,128)S(1)}, u32[]{:S(2)}, u32[]{:S(2)}) collective-permute-start(f32[4,1536]{1,0:T(4,128)S(1)} %slice.12), channel_id=1, source_target_pairs={{0,6},{1,7},{2,8},{3,9},{4,10},{5,11},{6,12},{7,13},{8,14},{9,15},... | collective-permute-start | bytes 73736
  1070.1 10.8 collective-permute-start
  1071.7 9.3 collective-permute-start.1
  1073.9 7.0 collective-permute-start.2
  1075.6 5.4 collective-permute-start.3
  1077.9 4.5 collective-permute-start.4
Sparse Core Ops, SparseCore 0:
  11.1 77.8 all-gather.27
  92.0 67.8 all-gather.25
  162.9 66.5 all-gather.17
  232.3 74.9 all-gather.21
  310.2 71.6 all-gather.29
  384.7 66.2 all-gather.19
  454.1 82.0 all-gather.15
  539.1 71.6 all-gather.13
  613.9 70.1 all-gather.23
  686.5 382.0 all-reduce.12
  1071.1 182.2 reduce-scatter.18
  1255.7 186.9 reduce-scatter.20
  1445.1 185.7 reduce-scatter.16
  1634.3 57.3 all-reduce.14
where the time goes:
time: 1710 us
  waiting for transfers between devices  1260 us (74%)
  blocking collectives  273 us (16%)
  matrix products  49.8 us (3%)
  starting transfers between devices  48.4 us (3%)
  local copies, waits for them, and re-layouts  45.6 us (3%)
    unnamed x30, waiting for transfers between devices  620 us
    unnamed x1, blocking collectives  273 us
    all_gather x3, waiting for transfers between devices, teacher_layer(): whole = lax.all_gather(projection, 'wide', axis=1, tiled=True)  208 us
    all_gather x3, waiting for transfers between devices, adaptor_grads(): lax.all_gather(first, 'wide', axis=0, tiled=True)  198 us
    all_gather x3, waiting for transfers between devices, adaptor_grads(): whole_second = lax.all_gather(second, 'wide', axis=0, tiled=True)  175 us
    psum x1, waiting for transfers between devices, body(): lax.psum((shards[0], shards[1], shards[2], shards[3], shards[4], shards[5...  60.7 us
    unnamed x16, starting transfers between devices  34.8 us
  transfers between devices with their start and end apart: 29, of which 15 were waited for; matrix products, arithmetic and copies ran while one was open for 22% of the time, Pallas kernels for 0%

commit v1 on v0

v1 whole, which is shorter than its diff:
```python
import functools
import itertools
import math

import jax
import jax.numpy as jnp
from jax import lax
from jax.experimental import pallas as pl
from jax.experimental.pallas import tpu as pltpu
from jax.sharding import PartitionSpec as P

MESH = pl.DeviceIdType.MESH
LANE = 128
ALL = (0, 4)
BOTH = (0, 2)


def layer_norm(values, count=None, mask=None):
    count = values.shape[-1] if count is None else count
    centered = values - jnp.sum(values, axis=-1, keepdims=True) * (1.0 / count)
    if mask is not None:
        centered = centered * mask
    variance = jnp.sum(centered * centered, axis=-1, keepdims=True) * (1.0 / count)
    return centered * lax.rsqrt(variance + 1e-05)


def gelu_pair(act):
    cdf = 0.5 * (1.0 + jax.scipy.special.erf(act * (1.0 / math.sqrt(2.0))))
    density = jnp.exp(-0.5 * act * act) * (1.0 / math.sqrt(2.0 * math.pi))
    return (act * cdf, cdf + act * density)


class Place:
    def __init__(self):
        grp, wide = lax.axis_index("grp"), lax.axis_index("wide")
        self.grp, self.wide = grp, wide
        self.z_lo, self.core = grp // 2, grp % 2
        self.y, self.x, self.z_hi = wide // 8, wide // 2 % 4, wide % 2

    def x_next(self, step):
        return (self.grp, (self.y * 4 + self.x_at(step)) * 2 + self.z_hi)

    def y_next(self, step):
        return (self.grp, (self.y_at(step) * 4 + self.x) * 2 + self.z_hi)

    def x_at(self, step):
        return (self.x + step + 4) % 4

    def y_at(self, step):
        return (self.y + step + 4) % 4

    def mirror_z(self):
        return ((1 - self.z_lo) * 2 + self.core, (self.y * 4 + self.x) * 2 + 1 - self.z_hi)

    def next_z(self):
        return ((1 - self.z_lo) * 2 + self.core, self.wide)

    def sibling(self):
        return (self.z_lo * 2 + 1 - self.core, self.wide)


def enter(partners):
    barrier = pltpu.get_barrier_semaphore()
    for partner in partners:
        pl.semaphore_signal(barrier, inc=1, device_id=partner, device_id_type=MESH)
    pl.semaphore_wait(barrier, len(partners))


def part(entry):
    return pl.ds(entry[0], entry[1]) if isinstance(entry, tuple) else entry


def extent(entry):
    return entry[1] if isinstance(entry, tuple) else None


class Copies:
    def __init__(self, send_sem, recv_sem):
        self.numbers = itertools.count()
        self.send_sem, self.recv_sem = send_sem, recv_sem
        self.started = []

    def send(self, src, dst, device):
        i = next(self.numbers)
        copy = pltpu.make_async_remote_copy(
            src_ref=src,
            dst_ref=dst,
            send_sem=self.send_sem.at[i],
            recv_sem=self.recv_sem.at[i],
            device_id=device,
            device_id_type=MESH,
        )
        copy.start()
        self.started.append(copy)
        return copy

    def finish(self):
        for copy in self.started:
            copy.wait_send()


def take_turns(streams):
    streams = list(streams)
    while streams:
        streams = [stream for stream in streams if next(stream, None) is not None]


def gather_kernel(splits, *refs):
    count = len(splits)
    ins, outs = refs[:count], refs[count : 2 * count]
    local_sem, send_sem, recv_sem = refs[2 * count :]
    at = Place()
    enter(
        [
            at.x_next(1),
            at.x_next(-1),
            at.y_next(1),
            at.y_next(-1),
            at.mirror_z(),
            at.sibling(),
        ]
    )
    copies = Copies(send_sem, recv_sem)
    halves = []

    def lanes(k, s):
        start = at.core * sum(splits[k]) + sum(splits[k][:s])
        return pl.ds(pl.multiple_of(start * LANE, LANE), splits[k][s] * LANE)

    def view(k, s, region):
        return outs[k].at[part(region[0]), part(region[1]), part(region[2]), :, lanes(k, s)]

    own = (at.y, at.x, at.z_hi)
    kept = [
        pltpu.make_async_copy(ins[k], outs[k].at[at.y, at.x, at.z_hi], local_sem.at[k])
        for k in range(count)
    ]
    for copy in kept:
        copy.start()

    def send(s, region, device, ks=None):
        ks = range(count) if ks is None else ks
        return [
            copies.send(
                ins[k].at[:, lanes(k, s)] if region is own else view(k, s, region),
                view(k, s, region),
                device,
            )
            for k in ks
        ]

    def arrived(s, sent, region, ks=None):
        for copy in sent:
            copy.wait_recv()
        halves.extend(send(s, region, at.sibling(), ks))

    def across(s, block):
        sent = send(s, block(at.z_hi), at.mirror_z())
        yield True
        arrived(s, sent, block(1 - at.z_hi))

    def around(s, block, place, device, cut=None):
        up = send(s, block(place(0)), device(1))
        down = send(s, block(place(0)), device(-1))
        yield True
        even, odd = range(0, count, 2), range(1, count, 2)
        arrived(s, up, block(place(-1)))
        if cut is None:
            up = send(s, block(place(-1)), device(1), even)
        else:
            up = send(s, cut(block(place(-1)), 0), device(1))
        arrived(s, down, block(place(1)))
        if cut is None:
            down = send(s, block(place(1)), device(-1), odd)
        else:
            down = send(s, cut(block(place(1)), 1), device(-1))
        yield True
        if cut is None:
            arrived(s, up, block(place(2)), even)
            arrived(s, down, block(place(2)), odd)
        else:
            arrived(s, up, cut(block(place(2)), 0))
            arrived(s, down, cut(block(place(2)), 1))

    def cut_y(region, half):
        return ((half * 2, 2), region[1], region[2])

    def cut_x(region, half):
        return (region[0], (half * 2, 2), region[2])

    def cut_z(region, half):
        return (region[0], region[1], half)

    def first_stream():
        yield from across(0, lambda c: own if c is at.z_hi else (at.y, at.x, c))
        yield from around(0, lambda c: (c, at.x, BOTH), at.y_at, at.y_next, cut_z)
        yield from around(0, lambda c: (ALL, c, BOTH), at.x_at, at.x_next, cut_y)

    def second_stream():
        yield from around(1, lambda c: (at.y, c, at.z_hi), at.x_at, at.x_next)
        yield from across(1, lambda c: (at.y, ALL, c))
        yield from around(1, lambda c: (c, ALL, BOTH), at.y_at, at.y_next, cut_x)

    def third_stream():
        yield from around(2, lambda c: (c, at.x, at.z_hi), at.y_at, at.y_next)
        yield from around(2, lambda c: (ALL, c, at.z_hi), at.x_at, at.x_next, cut_y)
        yield from across(2, lambda c: (ALL, ALL, c))

    for copy in kept:
        copy.wait()
    take_turns([first_stream(), second_stream(), third_stream()])
    for copy in halves:
        copy.wait_recv()
    copies.finish()


def gather(shards, splits):
    outs = [jax.ShapeDtypeStruct((4, 4, 2) + shard.shape, shard.dtype) for shard in shards]
    whole = pl.BlockSpec(memory_space=pl.ANY)
    semaphores = pltpu.SemaphoreType.DMA((52 * len(shards),))
    gathered = pl.pallas_call(
        functools.partial(gather_kernel, splits),
        out_shape=outs,
        in_specs=[whole] * len(shards),
        out_specs=[whole] * len(shards),
        scratch_shapes=[pltpu.SemaphoreType.DMA((len(shards),)), semaphores, semaphores],
        compiler_params=pltpu.CompilerParams(collective_id=0, has_side_effects=True),
        name="gather_weights",
    )(*shards)
    return [g.reshape(-1, g.shape[-1]) for g in gathered]


def reduce_kernel(splits, *refs):
    count = len(splits)
    ins, outs = refs[:count], refs[count : 2 * count]
    sums, last = refs[2 * count : 3 * count], refs[3 * count : 4 * count]
    spare, (send_sem, recv_sem) = refs[4 * count : -2], refs[-2:]
    at = Place()
    enter(
        [
            at.x_next(1),
            at.x_next(-1),
            at.y_next(1),
            at.y_next(-1),
            at.mirror_z(),
            at.next_z(),
            at.sibling(),
        ]
    )
    copies = Copies(send_sem, recv_sem)
    numbers = itertools.count()

    def lanes(k, s):
        return pl.ds(sum(splits[k][:s]) * LANE, splits[k][s] * LANE)

    def wide_lanes(k, s, core):
        start = core * sum(splits[k]) + sum(splits[k][:s])
        return pl.ds(pl.multiple_of(start * LANE, LANE), splits[k][s] * LANE)

    def view(k, s, region):
        return sums[k].at[part(region[0]), part(region[1]), part(region[2]), :, lanes(k, s)]

    def send(s, region, device, ks=None):
        sent = []
        for k in range(count) if ks is None else ks:
            room = spare[next(numbers)]
            sent.append((k, room, copies.send(view(k, s, region), room, device)))
        return sent

    def add(s, sent, region):
        for k, room, copy in sent:
            copy.wait_recv()
            sizes = [extent(entry) for entry in region]
            steps = [size or 1 for size in sizes]

            @pl.loop(0, steps[0] * steps[1] * steps[2])
            def _(i, k=k, room=room, sizes=sizes, steps=steps):
                spots = (i // (steps[1] * steps[2]), i // steps[2] % steps[1], i % steps[2])
                there = tuple(spot for spot, size in zip(spots, sizes) if size)
                here = tuple(
                    spot + entry[0] if size else entry
                    for spot, size, entry in zip(spots, sizes, region)
                )
                where = here + (slice(None), lanes(k, s))
                sums[k][where] = sums[k][where] + room[there + (slice(None), slice(None))]

    def across(s, block):
        sent = send(s, block(1 - at.z_hi), at.mirror_z())
        yield True
        add(s, sent, block(at.z_hi))

    def around(s, block, place, device, cut=None):
        even, odd = range(0, count, 2), range(1, count, 2)
        if cut is None:
            up = send(s, block(place(2)), device(1), even)
            down = send(s, block(place(2)), device(-1), odd)
        else:
            up = send(s, cut(block(place(2)), 0), device(1))
            down = send(s, cut(block(place(2)), 1), device(-1))
        yield True
        add(s, up, block(place(1)) if cut is None else cut(block(place(1)), 0))
        up = send(s, block(place(1)), device(1))
        add(s, down, block(place(-1)) if cut is None else cut(block(place(-1)), 1))
        down = send(s, block(place(-1)), device(-1))
        yield True
        add(s, up, block(place(0)))
        add(s, down, block(place(0)))

    def cut_y(region, half):
        return ((half * 2, 2), region[1], region[2])

    def cut_x(region, half):
        return (region[0], (half * 2, 2), region[2])

    def cut_z(region, half):
        return (region[0], region[1], half)

    chip = [
        [
            copies.send(
                ins[k].at[:, :, :, :, wide_lanes(k, s, 1 - at.core)],
                sums[k].at[:, :, :, :, lanes(k, s)],
                at.sibling(),
            )
            for k in range(count)
        ]
        for s in range(3)
    ]

    def join(s):
        for k in range(count):
            chip[s][k].wait_recv()

            @pl.loop(0, 32)
            def _(i, k=k):
                spot = (i // 8, i // 2 % 4, i % 2, slice(None))
                mine = ins[k][spot + (wide_lanes(k, s, at.core),)]
                sums[k][spot + (lanes(k, s),)] = sums[k][spot + (lanes(k, s),)] + mine

    def first_stream():
        join(0)
        yield from around(0, lambda c: (ALL, c, BOTH), at.x_at, at.x_next, cut_y)
        yield from around(0, lambda c: (c, at.x, BOTH), at.y_at, at.y_next, cut_z)
        yield from across(0, lambda c: (at.y, at.x, c))

    def second_stream():
        join(1)
        yield from around(1, lambda c: (c, ALL, BOTH), at.y_at, at.y_next, cut_x)
        yield from across(1, lambda c: (at.y, ALL, c))
        yield from around(1, lambda c: (at.y, c, at.z_hi), at.x_at, at.x_next)

    def third_stream():
        join(2)
        yield from across(2, lambda c: (ALL, ALL, c))
        yield from around(2, lambda c: (ALL, c, at.z_hi), at.x_at, at.x_next, cut_y)
        yield from around(2, lambda c: (c, at.x, at.z_hi), at.y_at, at.y_next)

    take_turns([first_stream(), second_stream(), third_stream()])
    own = (at.y, at.x, at.z_hi)
    pairs = [copies.send(sums[k].at[own], last[k], at.next_z()) for k in range(count)]
    halves = []
    for k in range(count):
        pairs[k].wait_recv()
        outs[k][at.core] = sums[k][own] + last[k][...]
        halves.append(copies.send(outs[k].at[at.core], outs[k].at[at.core], at.sibling()))
    for copy in halves:
        copy.wait_recv()
    copies.finish()


def spare_shapes(rows, splits):
    count = len(rows)

    def room(k, s, lead):
        return pltpu.VMEM(lead + (rows[k], splits[k][s] * LANE), jnp.float32)

    def across(s, lead):
        yield [room(k, s, lead) for k in range(count)]

    def around(s, lead, half=None):
        if half is None:
            yield [room(k, s, lead) for k in range(0, count, 2)] + [
                room(k, s, lead) for k in range(1, count, 2)
            ]
        else:
            yield [room(k, s, half) for k in range(count)] * 2
        yield [room(k, s, lead) for k in range(count)] * 2

    streams = [
        itertools.chain(around(0, (4, 2), (2, 2)), around(0, (2,), ()), across(0, ())),
        itertools.chain(around(1, (4, 2), (2, 2)), across(1, (4,)), around(1, ())),
        itertools.chain(across(2, (4, 4)), around(2, (4,), (2,)), around(2, ())),
    ]
    shapes = []
    while streams:
        left = []
        for stream in streams:
            group = next(stream, None)
            if group is not None:
                shapes.extend(group)
                left.append(stream)
        streams = left
    return shapes


def reduce_sum(partials, splits):
    count = len(partials)
    rows = [p.shape[-2] for p in partials]
    width = [p.shape[-1] // 2 for p in partials]
    inside = pl.BlockSpec(memory_space=pltpu.VMEM)
    semaphores = pltpu.SemaphoreType.DMA((32 * count,))
    out = pl.pallas_call(
        functools.partial(reduce_kernel, splits),
        out_shape=[
            jax.ShapeDtypeStruct((2, r, w), jnp.float32) for r, w in zip(rows, width)
        ],
        in_specs=[inside] * count,
        out_specs=[inside] * count,
        scratch_shapes=[pltpu.VMEM((4, 4, 2, r, w), jnp.float32) for r, w in zip(rows, width)]
        + [pltpu.VMEM((r, w), jnp.float32) for r, w in zip(rows, width)]
        + spare_shapes(rows, splits)
        + [semaphores, semaphores],
        compiler_params=pltpu.CompilerParams(
            collective_id=1, has_side_effects=True, vmem_limit_bytes=62 * 1024 * 1024
        ),
        name="reduce_gradients",
    )(*partials)
    return [jnp.concatenate([o[0], o[1]], axis=-1) for o in out]


def spread(width, group, room):
    rows = lax.broadcasted_iota(jnp.int32, (width, width // group * room), 0)
    columns = lax.broadcasted_iota(jnp.int32, (width, width // group * room), 1)
    return (rows // group * room + rows % group == columns).astype(jnp.bfloat16)


def place_columns(values, table):
    return jnp.dot(values, table, preferred_element_type=jnp.float32).astype(jnp.bfloat16)


def teacher_map(rows, projection, count=None, mask=None):
    mixed = lax.dot_general(
        rows, projection, (((1,), (1,)), ((), ())), preferred_element_type=jnp.float32
    )
    return layer_norm(rows.astype(jnp.float32) + mixed, count, mask).astype(jnp.bfloat16)


def pool_blocks(maps):
    held = lax.optimization_barrier(maps)
    blocks = held.astype(jnp.float32).reshape(maps.shape[0] // 4, 4, maps.shape[1])
    return jnp.mean(blocks, axis=1).astype(jnp.bfloat16)


def adaptor_grads(normed, target, first, second, factor):
    act = jnp.dot(normed, first, preferred_element_type=jnp.float32)
    hid_full, slope = gelu_pair(act)
    hidden = hid_full.astype(jnp.bfloat16)
    pred = jnp.dot(hidden, second, preferred_element_type=jnp.float32)
    grad_pred = (factor * (pred - target.astype(jnp.float32))).astype(jnp.bfloat16)
    grad_hid = lax.dot_general(
        grad_pred, second, (((1,), (1,)), ((), ())), preferred_element_type=jnp.float32
    )
    grad_act = (grad_hid * slope).astype(jnp.bfloat16)
    first_part = lax.dot_general(
        normed, grad_act, (((0,), (0,)), ((), ())), preferred_element_type=jnp.float32
    )
    second_part = lax.dot_general(
        hidden, grad_pred, (((0,), (0,)), ((), ())), preferred_element_type=jnp.float32
    )
    return (first_part, second_part)


def student_rows(student_feats, indices):
    normed = layer_norm(student_feats[0].astype(jnp.float32)).astype(jnp.bfloat16)
    patches = jnp.arange(256, dtype=jnp.int32)
    flags = jnp.stack([index[0] == patches for index in indices], axis=-1).astype(jnp.bfloat16)
    rows = jnp.concatenate([normed, jnp.pad(flags, ((0, 0), (0, LANE - 3)))], axis=-1)
    grid = rows.reshape(16, 16, -1)
    return jnp.concatenate(
        [grid.reshape(32, 8, -1), grid[:, ::-1].reshape(32, 8, -1)], axis=1
    )


def body(
    student_feats,
    dino_in,
    siglip_in,
    sam_in,
    dino_proj,
    siglip_proj,
    sam_proj,
    dino_index,
    siglip_index,
    sam_index,
    dino_first,
    dino_second,
    siglip_first,
    siglip_second,
    sam_first,
    sam_second,
):
    images_total = student_feats.shape[0] * 128
    rows = lax.all_to_all(
        student_rows(student_feats, (dino_index, siglip_index, sam_index)),
        "wide",
        split_axis=0,
        concat_axis=0,
        tiled=True,
    )
    width = student_feats.shape[-1]
    siglip_room = spread(1152, 36, 40)
    hidden_room = spread(640, 20, 24)
    siglip_turned = jnp.pad(place_columns(siglip_proj.T, siglip_room), ((0, 4), (0, 0)))
    firsts = place_columns(
        jnp.concatenate([dino_first, siglip_first, sam_first], axis=0), hidden_room
    ).reshape(3, 40, 768)
    seconds = jnp.concatenate(
        [dino_second, place_columns(siglip_second, siglip_room), sam_second], axis=1
    )
    dino_all, mixed_all, second_all = gather(
        [
            dino_proj.T,
            jnp.concatenate([sam_proj.T, siglip_turned, *firsts], axis=1),
            jnp.pad(seconds, ((0, 4), (0, 0))),
        ],
        ((2, 2, 2), (7, 7, 5), (6, 6, 4)),
    )
    sam_all, siglip_all, first_all = jnp.split(mixed_all, [1280, 2560], axis=1)

    siglip_mask = (jnp.arange(1280) % 40 < 36).astype(jnp.float32)
    targets = (
        teacher_map(dino_in.reshape(256, -1), dino_all),
        teacher_map(
            place_columns(siglip_in.reshape(256, -1), siglip_room), siglip_all, 1152, siglip_mask
        ),
        pool_blocks(teacher_map(sam_in.reshape(1024, -1), sam_all)),
    )
    factor = 2.0 / images_total
    straight, mirrored = rows[:, :8, :width], rows[:, 8:, :width]
    first_parts, second_parts = [], []
    for t, (target, begin, end) in enumerate(
        zip(targets, (0, 1536, 2816), (1536, 2816, 4096))
    ):
        flag = rows[:, :8, width + t : width + t + 1] > 0
        normed = jnp.where(flag, straight, mirrored).reshape(256, width)
        one, two = adaptor_grads(
            normed,
            target,
            first_all[:, t * 768 : (t + 1) * 768],
            second_all[:, begin:end],
            factor,
        )
        first_parts.append(one)
        second_parts.append(two)
    first_sum, second_sum = reduce_sum(
        [
            jnp.concatenate(first_parts, axis=1).reshape(4, 4, 2, 40, 2304),
            jnp.concatenate(second_parts, axis=1).reshape(4, 4, 2, 24, 4096),
        ],
        ((3, 3, 3), (6, 6, 4)),
    )
    firsts = first_sum.reshape(40, 3, 32, 24)[..., :20].reshape(40, 3, 640)
    seconds = second_sum[:20]
    siglip_two = seconds[:, 1536:2816].reshape(20, 32, 40)[..., :36].reshape(20, 1152)
    return (
        firsts[:, 0],
        seconds[:, :1536],
        firsts[:, 1],
        siglip_two,
        firsts[:, 2],
        seconds[:, 2816:],
    )


def solution(mesh):
    shared = P("wide", None)
    return jax.shard_map(
        body,
        mesh=mesh,
        in_specs=(
            P(("grp", "wide"), None, None),
            *[P("grp", "wide", None)] * 3,
            *[P(None, "wide")] * 3,
            *[P(("grp", "wide"), None)] * 3,
            *[shared] * 6,
        ),
        out_specs=(shared,) * 6,
        check_vma=False,
    )
```

time: 1710 us -> 375 us (0.22)
  waiting for transfers between devices: 1260 us -> 0.01 us
  blocking collectives: 273 us -> 0 us
  Pallas kernels: 0 us -> 223 us
  starting transfers between devices: 48.4 us -> 11.3 us
  other arithmetic: 13.9 us -> 37.1 us
    unnamed x30 -> x0, waiting for transfers between devices: 620 us -> none
    all_gather x9 -> x0, waiting for transfers between devices: 581 us -> none  [the longest x3 208 us: teacher_layer(): whole = lax.all_gather(projection, 'wide', axis=1, tiled=True)]
    unnamed x1 -> x0, blocking collectives: 273 us -> none
    pallas_call x0 -> x2, Pallas kernels: none -> 223 us  [the longest x1 117 us: gather(): pl.pallas_call(functools.partial(gather_kernel, splits), out_shape=outs,...]
    psum x1 -> x0, waiting for transfers between devices: 60.7 us -> none  [body(): lax.psum((shards[0], shards[1], shards[2], shards[3], shards[4], shards[5...]
    unnamed x16 -> x0, starting transfers between devices: 34.8 us -> none
    concatenate x0 -> x5, other arithmetic: none -> 22.9 us  [the longest x1 10.5 us: body(): jnp.concatenate(first_parts, axis=1).reshape(4, 4, 2, 40, 2304)]
    unnamed x42 -> x56, local copies, waits for them, and re-layouts: 28.1 us -> 9.32 us
  transfers between devices with their start and end apart: 29 -> 1, of which waited for: 15 -> 0; matrix products, arithmetic and copies ran while one was open for 22% -> 12% of each run, Pallas kernels for 0% -> 31%
where the time goes in v1:
time: 375 us; the launch traced here: 374 us
  Pallas kernels  223 us (59%)
  matrix products  57.9 us (15%)
  local copies, waits for them, and re-layouts  43.1 us (11%)
  other arithmetic  37.1 us (10%)
  starting transfers between devices  11.3 us (3%)
    pallas_call x1, Pallas kernels, gather(): pl.pallas_call(functools.partial(gather_kernel, splits), out_shape=outs,...  117 us
    pallas_call x1, Pallas kernels, reduce_sum(): pl.pallas_call(functools.partial(reduce_kernel, splits), out_shape=[jax.S...  106 us
    dot_general x3, matrix products, adaptor_grads(): lax.dot_general(normed, grad_act, (((0,), (0,)), ((), ())), preferred_ele...  17.3 us
    concatenate x1, local copies, waits for them, and re-layouts, body(): jnp.concatenate(first_parts, axis=1).reshape(4, 4, 2, 40, 2304)  13.6 us
    dot_general x3, matrix products, teacher_map(): lax.dot_general(rows, projection, (((1,), (1,)), ((), ())), preferred_ele...  13.5 us
    all_to_all x1, starting transfers between devices, body(): lax.all_to_all(student_rows(student_feats, (dino_index, siglip_index, sam...  11.3 us
    concatenate x1, other arithmetic, body(): jnp.concatenate(first_parts, axis=1).reshape(4, 4, 2, 40, 2304)  10.5 us
    reshape x2, local copies, waits for them, and re-layouts, pool_blocks(): held.astype(jnp.float32).reshape(maps.shape[0] // 4, 4, maps.shape[1])  10.5 us
  transfers between devices with their start and end apart: 1, of which 0 were waited for; matrix products, arithmetic and copies ran while one was open for 12% of the time, Pallas kernels for 31%

profile of v1, /device:TPU:1, one launch (start us, length us, event | category | flops | bytes accessed | tf_op | source)
XLA Modules:
  0.0 373.6 jit_solution(9678008484773276881)
XLA Ops:
  0.6 0.7 bitcast_compare_fusion.2
  1.4 1.3 convert_reduce_fusion
  2.7 1.4 fusion.34
  4.1 0.7 bitcast_compare_fusion
  4.9 1.4 fusion.35
  6.5 0.6 rev.3
  7.1 1.3 pad_maximum_fusion.2
  8.4 11.3 %all-to-all-start = ((bf16[32,16,1408]{2,1,0:T(8,128)(2,1)}), bf16[32,16,1408]{2,1,0:T(8,128)(2,1)}, u32[]{:S(2)}, u32[]{:S(2)}) async-start(bf16[32,16,1408]{2,1,0:T(8,128)(2,1)} %pad_maximum_fusion.2), calls=%async_computation | async-start | bytes 2883584 | tf_op jit(solution)/shard_map/all_to_all | solution.py:503
  19.8 1.4 fusion.14
  21.2 1.4 fusion.13
  22.6 0.7 bitcast_dynamic-update-slice_fusion
  23.3 0.7 pad_dynamic-update-slice_fusion
  23.9 0.8 fusion.63
  24.8 0.7 slice_dynamic-update-slice_fusion.2
  25.5 0.7 slice_dynamic-update-slice_fusion.1
  26.1 0.6 slice_dynamic-update-slice_fusion.refs_1_
  26.8 2.5 convolution_convert_fusion
  29.3 2.7 copy.77
  32.0 0.7 fusion.104.refs_2_
  32.7 117.4 %gather_weights.1 = (bf16[4,4,2,48,1536]{4,3,2,1,0:T(8,128)(2,1)}, bf16[4,4,2,40,4864]{4,3,2,1,0:T(8,128)(2,1)}, bf16[4,4,2,24,4096]{4,3,2,1,0:T(8,128)(2,1)}) custom-call(bf16[48,1536]{1,0:T(8,128)(2,1)} %bitcast.110, bf16[40,4864]{1,0:T(8,128)(2,1)} %slice_dynamic-update-slice_fusion.refs_1_, bf16[24,4096]{1,0:T(8,128)(2,1)} %fusion.104.refs_2_), custom_call_target="tpu_custom_call" | custom-call | tf_op jit(solution)/shard_map/gather_weights/pallas_call | solution.py:221
  150.1 3.6 fusion.142
  153.7 6.1 %fusion.141 = (f32[1024]{0:T(1024)S(1)}, f32[1024,1280]{0,1:T(8,128)S(1)}) fusion(bf16[1024,1280]{1,0:T(8,128)(2,1)S(1)} %bitcast.108, bf16[1280,4864]{1,0:T(8,128)(2,1)} %bitcast.112, bf16[1024,1280]{0,1:T(8,128)(2,1)S(1)} %copy-done.3), kind=kOutput, calls=%fused_computation.195 | convolution fusion | flops 3359374336 | bytes 13766656 | tf_op jit(solution)/shard_map/dot_general | solution.py:442
  159.9 0.6 multiply_reduce_fusion
  160.5 0.8 multiply_convert_fusion
  161.3 0.3 multiply_reduce_fusion.2
  161.6 3.4 copy.78
  165.0 7.1 %reshape.198 = f32[256,4,1280]{2,1,0:T(4,128)} reshape(f32[1024,1280]{1,0:T(8,128)} %copy.78) | data formatting | bytes 10485760 | tf_op jit(solution)/shard_map/reshape | solution.py:450
  172.1 5.7 %reduce_sum.89 = f32[256,1280]{1,0:T(8,128)S(1)} reduce(f32[256,4,1280]{2,1,0:T(4,128)} %reshape.198, f32[]{:T(128)} %constant.34.clone.1), dimensions={1}, to_apply=%region_8.9 | reduce | flops 983040 | bytes 6553604 | tf_op jit(solution)/shard_map/reduce_sum | solution.py:451
  177.8 3.8 %fusion.143 = (f32[256]{0:T(256)S(1)}, f32[256,1536]{1,0:T(8,128)S(1)}) fusion(bf16[1536,1536]{1,0:T(8,128)(2,1)} %bitcast.124, bf16[32,8,1536]{2,1,0:T(8,128)(2,1)S(1)} %copy-done.15), kind=kOutput, calls=%fused_computation.197 | convolution fusion | flops 1209138944 | bytes 7078912 | tf_op jit(solution)/shard_map/dot_general | solution.py:442
  181.6 1.2 copy-done.4
  182.8 0.3 multiply_reduce_fusion.1
  183.1 1.1 fusion.139
  184.2 0.1 copy.86
  184.3 0.1 copy.87
  184.5 0.1 copy.88
  184.9 2.7 fusion.18
  187.7 2.4 fusion.12
  190.1 0.8 copy-done.11
  190.9 2.8 fusion.138
  193.7 2.8 fusion.20
  196.6 0.9 fusion.11
  197.4 0.8 copy-done.9
  198.3 2.7 fusion.137
  201.0 2.8 fusion.22
  203.9 0.9 fusion.10
  204.8 1.0 copy-done.8
  205.7 3.0 fusion.136
  208.7 5.5 %fusion.61 = f32[1280,768]{0,1:T(8,128)} fusion(bf16[256,1280]{1,0:T(8,128)(2,1)} %copy-done.11, bf16[768,4096]{1,0:T(8,128)(2,1)} %bitcast.117, f32[256,768]{1,0:T(8,128)S(1)} %fusion.18, pred[32,8]{1,0:T(8,128)(4,1)S(1)} %copy.76, bf16[32,16,1408]{2,1,0:T(8,128)(2,1)} %all-to-all-done), kind=kOutput, calls=%fused_computation.65 | convolution fusion | flops 1008926720 | bytes 8651008 | tf_op jit(solution)/shard_map/dot_general | solution.py:464
  214.2 6.4 %fusion.55 = f32[1280,768]{0,1:T(8,128)} fusion(bf16[256,1536]{1,0:T(8,128)(2,1)} %copy-done.8, bf16[768,4096]{1,0:T(8,128)(2,1)} %bitcast.118, f32[256,768]{1,0:T(8,128)S(1)} %fusion.22, pred[32,8]{1,0:T(8,128)(4,1)S(1)} %copy.70, bf16[32,16,1408]{2,1,0:T(8,128)(2,1)} %all-to-all-done), kind=kOutput, calls=%fused_computation.63 | convolution fusion | flops 1109590016 | bytes 9175296 | tf_op jit(solution)/shard_map/dot_general | solution.py:464
  220.6 5.4 %fusion.58 = f32[1280,768]{0,1:T(8,128)} fusion(bf16[256,1280]{1,0:T(8,128)(2,1)S(1)} %copy-done.10, bf16[768,4096]{1,0:T(8,128)(2,1)} %bitcast.119, f32[256,768]{1,0:T(8,128)S(1)} %fusion.20, pred[32,8]{1,0:T(8,128)(4,1)S(1)} %copy.73, bf16[32,16,1408]{2,1,0:T(8,128)(2,1)} %all-to-all-done), kind=kOutput, calls=%fused_computation.64 | convolution fusion | flops 1008926720 | bytes 8651008 | tf_op jit(solution)/shard_map/dot_general | solution.py:464
  226.0 10.5 %pad_maximum_fusion.1 = f32[1280,2304]{0,1:T(8,128)} fusion(f32[1280,768]{0,1:T(8,128)} %fusion.61, f32[1280,768]{0,1:T(8,128)} %fusion.58, f32[1280,768]{0,1:T(8,128)} %fusion.55), kind=kLoop, calls=%fused_computation.1 | loop fusion | flops 5898240 | bytes 23592960 | tf_op jit(solution)/shard_map/concatenate | solution.py:557
  236.5 13.6 %copy.79 = f32[1280,2304]{1,0:T(8,128)} copy(f32[1280,2304]{0,1:T(8,128)} %pad_maximum_fusion.1) | data formatting | bytes 23592960 | tf_op jit(solution)/shard_map/concatenate | solution.py:557
  250.1 10.4 %pad_maximum_fusion = f32[768,4096]{1,0:T(8,128)} fusion(f32[768,1280]{1,0:T(8,128)} %fusion.138, f32[768,1280]{1,0:T(8,128)} %fusion.137, f32[768,1536]{1,0:T(8,128)} %fusion.136), kind=kLoop, calls=%fused_computation | loop fusion | flops 6291456 | bytes 25165824 | tf_op jit(solution)/shard_map/concatenate | solution.py:558
  260.4 105.6 %reduce_gradients.1 = (f32[2,40,1152]{2,1,0:T(8,128)}, f32[2,24,2048]{2,1,0:T(8,128)}) custom-call(f32[4,4,2,40,2304]{4,3,2,1,0:T(8,128)} %bitcast.103, f32[4,4,2,24,4096]{4,3,2,1,0:T(8,128)} %bitcast.102), custom_call_target="tpu_custom_call" | custom-call | tf_op jit(solution)/shard_map/reduce_gradients/pallas_call | solution.py:412
  366.1 1.0 slice_bitcast_fusion.6
  367.1 1.0 slice_bitcast_fusion.3
  368.2 0.7 slice.117
  368.8 0.7 fusion.140
  369.5 0.2 reshape.195
  369.8 0.9 reshape.196
  370.7 0.4 copy.80
  371.2 0.8 copy.83
  372.0 0.8 copy.82
  372.8 0.8 copy.81
  (72 shorter events, 0.9 us)
Async XLA Ops:
  0.6 26.1 %copy-start = (bf16[32,8,1152]{2,1,0:T(8,128)(2,1)S(1)}, bf16[32,8,1152]{2,1,0:T(8,128)(2,1)}, u32[]{:S(2)}) copy-start(bf16[32,8,1152]{2,1,0:T(8,128)(2,1)} %param.18) | copy-start | bytes 1769476
  7.1 12.7 %copy-start.17 = (bf16[20,1152]{1,0:T(8,128)(2,1)S(1)}, bf16[20,1152]{1,0:T(8,128)(2,1)}, u32[]{:S(2)}) copy-start(bf16[20,1152]{1,0:T(8,128)(2,1)} %param.29) | copy-start | bytes 138244
  8.4 174.7 %all-to-all-start = ((bf16[32,16,1408]{2,1,0:T(8,128)(2,1)}), bf16[32,16,1408]{2,1,0:T(8,128)(2,1)}, u32[]{:S(2)}, u32[]{:S(2)}) async-start(bf16[32,16,1408]{2,1,0:T(8,128)(2,1)} %pad_maximum_fusion.2), calls=%async_computation | async-start | bytes 2883584 | tf_op jit(solution)/shard_map/all_to_all | solution.py:503
  19.8 1.4 copy-start.16
  21.2 1.4 copy-start.12
  21.2 2.8 copy-start.18
  21.2 2.7 copy-start.19
  21.2 2.7 copy-start.20
  26.8 2.5 copy-start.2
  29.3 2.7 copy-start.13
  29.3 2.7 copy-start.14
  150.1 3.6 copy-start.3
  153.7 7.6 %copy-start.6 = (f32[256,1280]{1,0:T(8,128)}, f32[256,1280]{1,0:T(8,128)S(1)}, u32[]{:S(2)}) copy-start(f32[256,1280]{1,0:T(8,128)S(1)} %get-tuple-element.57) | copy-start | bytes 3932164
  172.1 5.7 %copy-start.15 = (bf16[32,8,1536]{2,1,0:T(8,128)(2,1)S(1)}, bf16[32,8,1536]{2,1,0:T(8,128)(2,1)}, u32[]{:S(2)}) copy-start(bf16[32,8,1536]{2,1,0:T(8,128)(2,1)} %param.17) | copy-start | bytes 2359300
  181.6 1.2 copy-start.4
  187.7 8.9 %slice-start = ((s8[6291456]{0:T(1024)(128)(4,1)}), s8[4194304]{0:T(1024)(128)(4,1)S(1)}, s32[]{:S(2)}) async-start(s8[6291456]{0:T(1024)(128)(4,1)} %bitcast.120), calls=%async_computation.1 | async-start | bytes 8388608
  190.1 0.8 copy-start.11
  190.9 5.6 %slice-start.1 = ((s8[6291456]{0:T(1024)(128)(4,1)}), s8[2097152]{0:T(1024)(128)(4,1)S(1)}, s32[]{:S(2)}) async-start(s8[6291456]{0:T(1024)(128)(4,1)} %bitcast.120), calls=%async_computation.2 | async-start | bytes 4194304
  193.7 2.8 copy-start.7
  197.4 0.8 copy-start.9
  201.0 2.8 copy-start.5
  204.8 1.0 copy-start.8
  214.2 6.4 %copy-start.10 = (bf16[256,1280]{1,0:T(8,128)(2,1)S(1)}, bf16[256,1280]{1,0:T(8,128)(2,1)}, u32[]{:S(2)}) copy-start(bf16[256,1280]{1,0:T(8,128)(2,1)} %copy-done.9) | copy-start | bytes 1966084
  371.0 2.5 copy-start.1

commit v2 on v1

--- a/solution.py
+++ b/solution.py
@@ -99,16 +99,87 @@
             copy.wait_send()
 
 
+class Task:
+    def __init__(self, link, cost, needs, run, rank=0):
+        self.link, self.cost, self.run, self.rank = link, cost, run, rank
+        self.needs = [need for need in needs if need is not None]
+        self.copy, self.landed, self.done = None, False, None
+
+
+def plan(tasks):
+    free, now, order, left = {}, 0.0, [], list(tasks)
+    while left:
+        able = [
+            (max([need.done for need in task.needs], default=0.0), task)
+            for task in left
+            if all(need.done is not None for need in task.needs)
+        ]
+        soon = [pair for pair in able if pair[0] <= now]
+        if soon:
+            ready, task = min(soon, key=lambda pair: (pair[1].link == "core", pair[1].rank, pair[0]))
+        else:
+            ready, task = min(able, key=lambda pair: (pair[0], pair[1].rank))
+        now = max(now, ready)
+        if task.link == "core":
+            now += task.cost
+            task.done = now
+        else:
+            now += 0.15
+            rate = {"sibling": 0.4, "local": 0.4}.get(task.link, 0.0445)
+            free[task.link] = max(now, free.get(task.link, 0.0)) + task.cost * 1e-6 / rate
+            task.done = free[task.link] + 1.5
+        order.append(task)
+        left.remove(task)
+    return order
+
+
+def carry_out(order):
+    for task in order:
+        for need in task.needs:
+            land(need)
+        task.copy = task.run()
+    for task in order:
+        land(task)
+
+
+def land(task):
+    if task.copy is not None and not task.landed:
+        if task.link == "local":
+            task.copy.wait()
+        else:
+            task.copy.wait_recv()
+        task.landed = True
+
+
 def take_turns(streams):
     streams = list(streams)
     while streams:
         streams = [stream for stream in streams if next(stream, None) is not None]
 
 
+def cut_y(region, half):
+    return ((half * 2, 2), region[1], region[2])
+
+
+def cut_x(region, half):
+    return (region[0], (half * 2, 2), region[2])
+
+
+def cut_z(region, half):
+    return (region[0], region[1], half)
+
+
+def chunks(region):
+    return math.prod(extent(entry) or 1 for entry in region)
+
+
 def gather_kernel(splits, *refs):
     count = len(splits)
-    ins, outs = refs[:count], refs[count : 2 * count]
-    local_sem, send_sem, recv_sem = refs[2 * count :]
+    ins, refs = refs[:count], refs[count:]
+    (dino_in, siglip_in, sam_in), refs = refs[:3], refs[3:]
+    (first_out, second_out, dino_out, siglip_out, sam_out), refs = refs[:5], refs[5:]
+    dino_all, mixed_all, pre, cells, local_sem, send_sem, recv_sem = refs
+    outs = (dino_all, mixed_all, first_out, second_out)
     at = Place()
     enter(
         [
@@ -117,11 +188,12 @@
             at.y_next(1),
             at.y_next(-1),
             at.mirror_z(),
+            at.next_z(),
             at.sibling(),
         ]
     )
     copies = Copies(send_sem, recv_sem)
-    halves = []
+    tasks = []
 
     def lanes(k, s):
         start = at.core * sum(splits[k]) + sum(splits[k][:s])
@@ -130,104 +202,170 @@
     def view(k, s, region):
         return outs[k].at[part(region[0]), part(region[1]), part(region[2]), :, lanes(k, s)]
 
+    def keep(k):
+        def run():
+            copy = pltpu.make_async_copy(
+                ins[k], outs[k].at[at.y, at.x, at.z_hi], local_sem.at[k]
+            )
+            copy.start()
+            return copy
+
+        return Task("local", ins[k].shape[0] * ins[k].shape[1] * 2, [], run, k)
+
+    kept = [keep(k) for k in range(count)]
+    tasks.extend(kept)
+
+    def send(k, s, region, link, device, needs):
+        def run():
+            src = ins[k].at[:, lanes(k, s)] if region is own else view(k, s, region)
+            return copies.send(src, view(k, s, region), device)
+
+        size = chunks(region) * ins[k].shape[0] * splits[k][s] * LANE * 2
+        task = Task(link, size, needs, run, k)
+        tasks.append(task)
+        return task
+
     own = (at.y, at.x, at.z_hi)
-    kept = [
-        pltpu.make_async_copy(ins[k], outs[k].at[at.y, at.x, at.z_hi], local_sem.at[k])
-        for k in range(count)
-    ]
-    for copy in kept:
-        copy.start()
-
-    def send(s, region, device, ks=None):
-        ks = range(count) if ks is None else ks
-        return [
-            copies.send(
-                ins[k].at[:, lanes(k, s)] if region is own else view(k, s, region),
-                view(k, s, region),
-                device,
+    found = [[] for _ in range(count)]
+
+    def arrive(k, s, region, task):
+        half = send(k, s, region, "sibling", at.sibling(), [task])
+        found[k] += [task, half]
+        return task
+
+    def across(k, s, needs):
+        task = send(k, s, own, "mirror", at.mirror_z(), needs)
+        return [arrive(k, s, (at.y, at.x, 1 - at.z_hi), task)]
+
+    def across_both(k, s, needs):
+        first = send(k, s, ((2 - 2 * at.z_lo, 2), ALL, at.z_hi), "mirror", at.mirror_z(), needs)
+        here = ((2 * at.z_lo, 2), ALL, 1 - at.z_hi)
+        arrive(k, s, here, first)
+        second = send(k, s, here, "next", at.next_z(), [first])
+        arrive(k, s, ((2 - 2 * at.z_lo, 2), ALL, 1 - at.z_hi), second)
+
+    def around(k, s, axis, block, cut, needs):
+        place, device = (at.x_at, at.x_next) if axis == "x" else (at.y_at, at.y_next)
+        here = own if cut is None else block(place(0))
+        back, ahead, over = block(place(-1)), block(place(1)), block(place(2))
+        up = arrive(k, s, back, send(k, s, here, axis + "+", device(1), needs))
+        down = arrive(k, s, ahead, send(k, s, here, axis + "-", device(-1), needs))
+        got = [up, down]
+        if cut is not None:
+            task = send(k, s, cut(back, 0), axis + "+", device(1), [up])
+            got.append(arrive(k, s, cut(over, 0), task))
+            task = send(k, s, cut(ahead, 1), axis + "-", device(-1), [down])
+            got.append(arrive(k, s, cut(over, 1), task))
+        elif k % 2 == 0:
+            task = send(k, s, back, axis + "+", device(1), [up])
+            got.append(arrive(k, s, over, task))
+        else:
+            task = send(k, s, ahead, axis + "-", device(-1), [down])
+            got.append(arrive(k, s, over, task))
+        return got
+
+    for k in range(count):
+        mine = [kept[k]]
+        got = across(k, 0, [])
+        got = mine + got + around(k, 0, "y", lambda c: (c, at.x, BOTH), cut_z, mine + got)
+        around(k, 0, "x", lambda c: (ALL, c, BOTH), cut_y, got)
+        got = across(k, 1, [])
+        got = mine + got + around(k, 1, "x", lambda c: (at.y, c, BOTH), cut_z, mine + got)
+        around(k, 1, "y", lambda c: (c, ALL, BOTH), cut_x, got)
+        got = mine + around(k, 2, "x", lambda c: (at.y, c, at.z_hi), None, [])
+        got = got + around(k, 2, "y", lambda c: (c, ALL, at.z_hi), cut_x, got)
+        across_both(k, 2, got)
+        got = mine + around(k, 3, "y", lambda c: (c, at.x, at.z_hi), None, [])
+        got = got + around(k, 3, "x", lambda c: (ALL, c, at.z_hi), cut_y, got)
+        across_both(k, 3, got)
+
+    def mix(rows_ref, begin, weights, lane, width, count, mask, write):
+        rows = rows_ref[begin : begin + 256, :]
+        step = weights.shape[3] * 16
+        for half in range(2):
+            block = weights[2 * half : 2 * half + 2, :, :, :, lane : lane + rows.shape[1]]
+            mixed = lax.dot_general(
+                rows,
+                block.reshape(step, rows.shape[1]),
+                (((1,), (1,)), ((), ())),
+                preferred_element_type=jnp.float32,
             )
-            for k in ks
-        ]
-
-    def arrived(s, sent, region, ks=None):
-        for copy in sent:
-            copy.wait_recv()
-        halves.extend(send(s, region, at.sibling(), ks))
-
-    def across(s, block):
-        sent = send(s, block(at.z_hi), at.mirror_z())
-        yield True
-        arrived(s, sent, block(1 - at.z_hi))
-
-    def around(s, block, place, device, cut=None):
-        up = send(s, block(place(0)), device(1))
-        down = send(s, block(place(0)), device(-1))
-        yield True
-        even, odd = range(0, count, 2), range(1, count, 2)
-        arrived(s, up, block(place(-1)))
-        if cut is None:
-            up = send(s, block(place(-1)), device(1), even)
-        else:
-            up = send(s, cut(block(place(-1)), 0), device(1))
-        arrived(s, down, block(place(1)))
-        if cut is None:
-            down = send(s, block(place(1)), device(-1), odd)
-        else:
-            down = send(s, cut(block(place(1)), 1), device(-1))
-        yield True
-        if cut is None:
-            arrived(s, up, block(place(2)), even)
-            arrived(s, down, block(place(2)), odd)
-        else:
-            arrived(s, up, cut(block(place(2)), 0))
-            arrived(s, down, cut(block(place(2)), 1))
-
-    def cut_y(region, half):
-        return ((half * 2, 2), region[1], region[2])
-
-    def cut_x(region, half):
-        return (region[0], (half * 2, 2), region[2])
-
-    def cut_z(region, half):
-        return (region[0], region[1], half)
-
-    def first_stream():
-        yield from across(0, lambda c: own if c is at.z_hi else (at.y, at.x, c))
-        yield from around(0, lambda c: (c, at.x, BOTH), at.y_at, at.y_next, cut_z)
-        yield from around(0, lambda c: (ALL, c, BOTH), at.x_at, at.x_next, cut_y)
-
-    def second_stream():
-        yield from around(1, lambda c: (at.y, c, at.z_hi), at.x_at, at.x_next)
-        yield from across(1, lambda c: (at.y, ALL, c))
-        yield from around(1, lambda c: (c, ALL, BOTH), at.y_at, at.y_next, cut_x)
-
-    def third_stream():
-        yield from around(2, lambda c: (c, at.x, at.z_hi), at.y_at, at.y_next)
-        yield from around(2, lambda c: (ALL, c, at.z_hi), at.x_at, at.x_next, cut_y)
-        yield from across(2, lambda c: (ALL, ALL, c))
-
-    for copy in kept:
-        copy.wait()
-    take_turns([first_stream(), second_stream(), third_stream()])
-    for copy in halves:
-        copy.wait_recv()
+            side = rows[:, half * step : (half + 1) * step].astype(jnp.float32)
+            pre[:, half * step : (half + 1) * step] = side + mixed
+
+        @pl.loop(0, 8)
+        def _(i):
+            spot = pl.ds(pl.multiple_of(i * 32, 32), 32)
+            values = pre[spot, :width]
+            write(spot, layer_norm(values, count, mask).astype(jnp.bfloat16))
+
+    def dino():
+        def write(spot, values):
+            dino_out[spot, :] = values
+
+        mix(dino_in, 0, dino_all, 0, 1536, 1536, None, write)
+
+    def siglip():
+        def write(spot, values):
+            siglip_out[spot, :] = values
+
+        column = lax.broadcasted_iota(jnp.int32, (1, 1280), 1)
+        mask = (column % 40 < 36).astype(jnp.float32)
+        mix(siglip_in, 0, mixed_all, 1280, 1280, 1152, mask, write)
+
+    def sam(b):
+        def run():
+            def write(spot, values):
+                cells[spot, :] = values
+
+            mix(sam_in, b * 256, mixed_all, 0, 1280, 1280, None, write)
+            block = lax.broadcasted_iota(jnp.int32, (64, 256), 0)
+            cell = lax.broadcasted_iota(jnp.int32, (64, 256), 1)
+            member = ((cell >= 4 * block) & (cell < 4 * block + 4)).astype(jnp.bfloat16)
+            total = jnp.dot(member, cells[...], preferred_element_type=jnp.float32)
+            sam_out[b * 64 : b * 64 + 64, :] = (total * 0.25).astype(jnp.bfloat16)
+
+        return run
+
+    tasks.append(Task("core", 4.0, found[0] + [kept[0]], dino))
+    tasks.append(Task("core", 4.0, found[1] + [kept[1]], siglip))
+    for b in range(4):
+        tasks.append(Task("core", 3.5, found[1] + [kept[1]], sam(b)))
+    carry_out(plan(tasks))
     copies.finish()
 
 
-def gather(shards, splits):
-    outs = [jax.ShapeDtypeStruct((4, 4, 2) + shard.shape, shard.dtype) for shard in shards]
+def gather_and_map(shards, rows, splits):
     whole = pl.BlockSpec(memory_space=pl.ANY)
-    semaphores = pltpu.SemaphoreType.DMA((52 * len(shards),))
-    gathered = pl.pallas_call(
+    inside = pl.BlockSpec(memory_space=pltpu.VMEM)
+    shapes = [(4, 4, 2) + shard.shape for shard in shards]
+    semaphores = pltpu.SemaphoreType.DMA((72 * len(shards),))
+    first, second, dino, siglip, sam = pl.pallas_call(
         functools.partial(gather_kernel, splits),
-        out_shape=outs,
-        in_specs=[whole] * len(shards),
-        out_specs=[whole] * len(shards),
-        scratch_shapes=[pltpu.SemaphoreType.DMA((len(shards),)), semaphores, semaphores],
-        compiler_params=pltpu.CompilerParams(collective_id=0, has_side_effects=True),
-        name="gather_weights",
-    )(*shards)
-    return [g.reshape(-1, g.shape[-1]) for g in gathered]
+        out_shape=[
+            jax.ShapeDtypeStruct(shapes[2], jnp.bfloat16),
+            jax.ShapeDtypeStruct(shapes[3], jnp.bfloat16),
+            jax.ShapeDtypeStruct((256, 1536), jnp.bfloat16),
+            jax.ShapeDtypeStruct((256, 1280), jnp.bfloat16),
+            jax.ShapeDtypeStruct((256, 1280), jnp.bfloat16),
+        ],
+        in_specs=[whole] * len(shards) + [inside] * 3,
+        out_specs=[whole] * 2 + [inside] * 3,
+        scratch_shapes=[
+            pltpu.VMEM(shapes[0], jnp.bfloat16),
+            pltpu.VMEM(shapes[1], jnp.bfloat16),
+            pltpu.VMEM((256, 1536), jnp.float32),
+            pltpu.VMEM((256, 1280), jnp.bfloat16),
+            pltpu.SemaphoreType.DMA((len(shards),)),
+            semaphores,
+            semaphores,
+        ],
+        compiler_params=pltpu.CompilerParams(
+            collective_id=0, has_side_effects=True, vmem_limit_bytes=60 * 1024 * 1024
+        ),
+        name="gather_and_map",
+    )(*shards, *rows)
+    return [first.reshape(1280, -1), second.reshape(768, -1), dino, siglip, sam]
 
 
 def reduce_kernel(splits, *refs):
@@ -436,19 +574,6 @@
 
 def place_columns(values, table):
     return jnp.dot(values, table, preferred_element_type=jnp.float32).astype(jnp.bfloat16)
-
-
-def teacher_map(rows, projection, count=None, mask=None):
-    mixed = lax.dot_general(
-        rows, projection, (((1,), (1,)), ((), ())), preferred_element_type=jnp.float32
-    )
-    return layer_norm(rows.astype(jnp.float32) + mixed, count, mask).astype(jnp.bfloat16)
-
-
-def pool_blocks(maps):
-    held = lax.optimization_barrier(maps)
-    blocks = held.astype(jnp.float32).reshape(maps.shape[0] // 4, 4, maps.shape[1])
-    return jnp.mean(blocks, axis=1).astype(jnp.bfloat16)
 
 
 def adaptor_grads(normed, target, first, second, factor):
@@ -517,23 +642,19 @@
     seconds = jnp.concatenate(
         [dino_second, place_columns(siglip_second, siglip_room), sam_second], axis=1
     )
-    dino_all, mixed_all, second_all = gather(
+    first_all, second_all, *targets = gather_and_map(
         [
             dino_proj.T,
-            jnp.concatenate([sam_proj.T, siglip_turned, *firsts], axis=1),
+            jnp.concatenate([sam_proj.T, siglip_turned], axis=1),
+            jnp.concatenate([*firsts], axis=1),
             jnp.pad(seconds, ((0, 4), (0, 0))),
         ],
-        ((2, 2, 2), (7, 7, 5), (6, 6, 4)),
-    )
-    sam_all, siglip_all, first_all = jnp.split(mixed_all, [1280, 2560], axis=1)
-
-    siglip_mask = (jnp.arange(1280) % 40 < 36).astype(jnp.float32)
-    targets = (
-        teacher_map(dino_in.reshape(256, -1), dino_all),
-        teacher_map(
-            place_columns(siglip_in.reshape(256, -1), siglip_room), siglip_all, 1152, siglip_mask
-        ),
-        pool_blocks(teacher_map(sam_in.reshape(1024, -1), sam_all)),
+        [
+            dino_in.reshape(256, -1),
+            place_columns(siglip_in.reshape(256, -1), siglip_room),
+            sam_in.reshape(1024, -1),
+        ],
+        ((1, 1, 2, 2), (2, 2, 3, 3), (2, 2, 3, 2), (3, 3, 5, 5)),
     )
     factor = 2.0 / images_total
     straight, mirrored = rows[:, :8, :width], rows[:, 8:, :width]

time: 375 us -> 299 us (0.80)
  Pallas kernels: 223 us -> 192 us
  local copies, waits for them, and re-layouts: 43.1 us -> 23.6 us
  matrix products: 57.9 us -> 39.3 us
  other arithmetic: 37.1 us -> 30.7 us
    pallas_call x1, Pallas kernels: 117 us -> 87.9 us  [gather_and_map(): pl.pallas_call(functools.partial(gather_kernel, splits), out_shape=[jax.S...]
    dot_general x3 -> x0, matrix products: 13.5 us -> none  [teacher_map(): lax.dot_general(rows, projection, (((1,), (1,)), ((), ())), preferred_ele...]
    reshape x3 -> x0, local copies, waits for them, and re-layouts: 13.2 us -> none  [the longest x2 10.5 us: pool_blocks(): held.astype(jnp.float32).reshape(maps.shape[0] // 4, 4, maps.shape[1])]
    reduce_sum x1 -> x0, other arithmetic: 5.66 us -> none  [pool_blocks(): return jnp.mean(blocks, axis=1).astype(jnp.bfloat16)]
    unnamed x56 -> x52, local copies, waits for them, and re-layouts: 9.32 us -> 4.56 us
    dot_general x3, matrix products: 8.39 us -> 4.02 us  [adaptor_grads(): act = jnp.dot(normed, first, preferred_element_type=jnp.float32)]
  transfers between devices with their start and end apart: 1 -> 1, of which waited for: 0 -> 0; matrix products, arithmetic and copies ran while one was open for 12% -> 3% of each run, Pallas kernels for 31% -> 30%
where the time goes in v2:
time: 299 us; the launch traced here: 298 us
  Pallas kernels  192 us (64%)
  matrix products  39.3 us (13%)
  other arithmetic  30.7 us (10%)
  local copies, waits for them, and re-layouts  23.6 us (8%)
  starting transfers between devices  11.2 us (4%)
    pallas_call x1, Pallas kernels, reduce_sum(): pl.pallas_call(functools.partial(reduce_kernel, splits), out_shape=[jax.S...  104 us
    pallas_call x1, Pallas kernels, gather_and_map(): pl.pallas_call(functools.partial(gather_kernel, splits), out_shape=[jax.S...  87.9 us
    dot_general x3, matrix products, adaptor_grads(): lax.dot_general(normed, grad_act, (((0,), (0,)), ((), ())), preferred_ele...  16.8 us
    concatenate x1, local copies, waits for them, and re-layouts, body(): jnp.concatenate(first_parts, axis=1).reshape(4, 4, 2, 40, 2304)  13.6 us
    all_to_all x1, starting transfers between devices, body(): lax.all_to_all(student_rows(student_feats, (dino_index, siglip_index, sam...  11.2 us
    concatenate x1, other arithmetic, body(): jnp.concatenate(first_parts, axis=1).reshape(4, 4, 2, 40, 2304)  10.5 us
    concatenate x1, other arithmetic, body(): jnp.concatenate(second_parts, axis=1).reshape(4, 4, 2, 24, 4096)  10.4 us
    dot_general x3, matrix products, adaptor_grads(): lax.dot_general(hidden, grad_pred, (((0,), (0,)), ((), ())), preferred_el...  8.37 us
  transfers between devices with their start and end apart: 1, of which 0 were waited for; matrix products, arithmetic and copies ran while one was open for 3% of the time, Pallas kernels for 30%

profile of v2, /device:TPU:1, one launch (start us, length us, event | category | flops | bytes accessed | tf_op | source)
XLA Modules:
  0.0 298.0 jit_solution(18306438532209947485)
XLA Ops:
  0.6 0.0 copy-start
  0.6 0.7 bitcast_compare_fusion.2
  1.4 1.3 convert_reduce_fusion
  2.7 1.4 fusion.28
  4.1 0.7 bitcast_compare_fusion
  4.8 0.1 copy.57
  4.9 1.4 fusion.29
  6.4 0.1 fusion.125
  6.5 0.6 rev.3
  7.1 0.0 copy-start.16
  7.1 0.0 copy-start.17
  7.1 0.0 copy-start.18
  7.1 1.2 pad_maximum_fusion.2
  8.3 11.2 %all-to-all-start = ((bf16[32,16,1408]{2,1,0:T(8,128)(2,1)}), bf16[32,16,1408]{2,1,0:T(8,128)(2,1)S(1)}, u32[]{:S(2)}, u32[]{:S(2)}) async-start(bf16[32,16,1408]{2,1,0:T(8,128)(2,1)} %pad_maximum_fusion.2), calls=%async_computation | async-start | bytes 2883584 | tf_op jit(solution)/shard_map/all_to_all | solution.py:628
  19.5 0.0 copy-start.14
  19.7 0.8 fusion.57
  20.5 0.0 copy-start.8
  20.6 0.0 copy-start.15
  20.6 1.4 fusion.7
  22.0 0.7 fusion.97.refs_1_
  22.7 0.7 pad_maximum_fusion.5.refs_2_
  23.4 1.3 fusion.8
  24.7 0.7 fusion.99.refs_3_
  25.4 2.5 fusion.6.refs_5_
  28.0 87.9 %gather_and_map.1 = (bf16[4,4,2,40,2304]{4,3,2,1,0:T(8,128)(2,1)}, bf16[4,4,2,24,4096]{4,3,2,1,0:T(8,128)(2,1)}, bf16[256,1536]{1,0:T(8,128)(2,1)}, bf16[256,1280]{1,0:T(8,128)(2,1)}, bf16[256,1280]{1,0:T(8,128)(2,1)}) custom-call(bf16[48,1536]{1,0:T(8,128)(2,1)} %bitcast.95, bf16[40,2560]{1,0:T(8,128)(2,1)} %fusion.97.refs_1_, ...), custom_call_target="tpu_custom_call" | custom-call | tf_op jit(solution)/shard_map/gather_and_map/pallas_call | solution.py:343
  115.9 0.1 fusion.129
  116.0 0.1 copy.71
  116.2 0.1 copy.72
  116.3 0.1 copy.73
  116.5 0.1 copy.64
  116.6 0.1 copy.62
  116.7 0.1 copy.59
  116.8 2.5 fusion.14
  119.3 2.4 fusion.4
  121.8 2.7 fusion.127
  124.5 0.8 fusion.12
  125.3 0.1 slice-done.1
  125.4 0.3 copy-done.12
  125.7 0.8 fusion.5
  126.5 2.7 fusion.128
  129.2 0.8 fusion.16
  130.0 0.4 copy-done.11
  130.4 0.8 fusion.3
  131.2 0.9 copy-done.4
  132.1 3.0 fusion.126
  135.1 5.5 %fusion.52 = f32[1280,768]{0,1:T(8,128)} fusion(bf16[256,1280]{1,0:T(8,128)(2,1)} %copy-done.7, bf16[768,4096]{1,0:T(8,128)(2,1)} %bitcast.98, f32[256,768]{1,0:T(8,128)S(1)} %fusion.14, pred[32,8]{1,0:T(8,128)(4,1)S(1)} %copy.62, bf16[32,16,1408]{2,1,0:T(8,128)(2,1)} %copy-done.2), kind=kOutput, calls=%fused_computation.50 | convolution fusion | flops 1008926720 | bytes 8651008 | tf_op jit(solution)/shard_map/dot_general | solution.py:589
  140.6 6.0 %fusion.49 = f32[1280,768]{0,1:T(8,128)} fusion(bf16[256,1536]{1,0:T(8,128)(2,1)} %copy-done.4, bf16[768,4096]{1,0:T(8,128)(2,1)} %bitcast.99, f32[256,768]{1,0:T(8,128)S(1)} %fusion.16, pred[32,8]{1,0:T(8,128)(4,1)S(1)} %copy.59, bf16[32,16,1408]{2,1,0:T(8,128)(2,1)} %copy-done.2), kind=kOutput, calls=%fused_computation.49 | convolution fusion | flops 1109590016 | bytes 9175296 | tf_op jit(solution)/shard_map/dot_general | solution.py:589
  146.5 5.3 %fusion.55 = f32[1280,768]{0,1:T(8,128)} fusion(bf16[256,1280]{1,0:T(8,128)(2,1)S(1)} %copy-done.6, bf16[768,4096]{1,0:T(8,128)(2,1)} %bitcast.100, f32[256,768]{1,0:T(8,128)S(1)} %fusion.12, pred[32,8]{1,0:T(8,128)(4,1)S(1)} %copy.64, bf16[32,16,1408]{2,1,0:T(8,128)(2,1)} %copy-done.2), kind=kOutput, calls=%fused_computation.51 | convolution fusion | flops 1008926720 | bytes 8651008 | tf_op jit(solution)/shard_map/dot_general | solution.py:589
  151.9 10.5 %pad_maximum_fusion.1 = f32[1280,2304]{0,1:T(8,128)} fusion(f32[1280,768]{0,1:T(8,128)} %fusion.55, f32[1280,768]{0,1:T(8,128)} %fusion.52, f32[1280,768]{0,1:T(8,128)} %fusion.49), kind=kLoop, calls=%fused_computation.1 | loop fusion | flops 5898240 | bytes 23592960 | tf_op jit(solution)/shard_map/concatenate | solution.py:678
  162.4 13.6 %copy.65 = f32[1280,2304]{1,0:T(8,128)} copy(f32[1280,2304]{0,1:T(8,128)} %pad_maximum_fusion.1) | data formatting | bytes 23592960 | tf_op jit(solution)/shard_map/concatenate | solution.py:678
  175.9 10.4 %pad_maximum_fusion = f32[768,4096]{1,0:T(8,128)} fusion(f32[768,1280]{1,0:T(8,128)} %fusion.128, f32[768,1280]{1,0:T(8,128)} %fusion.127, f32[768,1536]{1,0:T(8,128)} %fusion.126), kind=kLoop, calls=%fused_computation | loop fusion | flops 6291456 | bytes 25165824 | tf_op jit(solution)/shard_map/concatenate | solution.py:679
  186.3 104.2 %reduce_gradients.1 = (f32[2,40,1152]{2,1,0:T(8,128)}, f32[2,24,2048]{2,1,0:T(8,128)}) custom-call(f32[4,4,2,40,2304]{4,3,2,1,0:T(8,128)} %bitcast.88, f32[4,4,2,24,4096]{4,3,2,1,0:T(8,128)} %bitcast.87), custom_call_target="tpu_custom_call" | custom-call | tf_op jit(solution)/shard_map/reduce_gradients/pallas_call | solution.py:550
  290.5 1.0 slice_bitcast_fusion.6
  291.6 1.0 slice_bitcast_fusion.3
  292.6 0.7 slice.114
  293.3 0.7 fusion.130
  293.9 0.2 reshape.136
  294.2 0.9 reshape.137
  295.1 0.4 copy.66
  295.5 0.1 reshape.135
  295.6 0.1 slice_bitcast_fusion
  295.6 0.8 copy.69
  296.4 0.8 copy.68
  297.2 0.8 copy.67
  (53 shorter events, 0.2 us)
Async XLA Ops:
  0.6 24.8 %copy-start = (bf16[32,8,1152]{2,1,0:T(8,128)(2,1)S(1)}, bf16[32,8,1152]{2,1,0:T(8,128)(2,1)}, u32[]{:S(2)}) copy-start(bf16[32,8,1152]{2,1,0:T(8,128)(2,1)} %param.18) | copy-start | bytes 1769476
  7.1 12.6 %copy-start.16 = (bf16[40,640]{1,0:T(8,128)(2,1)S(1)}, bf16[40,640]{1,0:T(8,128)(2,1)}, u32[]{:S(2)}) copy-start(bf16[40,640]{1,0:T(8,128)(2,1)} %param.30) | copy-start | bytes 153604
  7.1 12.6 %copy-start.17 = (bf16[40,640]{1,0:T(8,128)(2,1)S(1)}, bf16[40,640]{1,0:T(8,128)(2,1)}, u32[]{:S(2)}) copy-start(bf16[40,640]{1,0:T(8,128)(2,1)} %param.28) | copy-start | bytes 153604
  7.1 12.6 %copy-start.18 = (bf16[40,640]{1,0:T(8,128)(2,1)S(1)}, bf16[40,640]{1,0:T(8,128)(2,1)}, u32[]{:S(2)}) copy-start(bf16[40,640]{1,0:T(8,128)(2,1)} %param.26) | copy-start | bytes 153604
  8.3 107.5 %all-to-all-start = ((bf16[32,16,1408]{2,1,0:T(8,128)(2,1)}), bf16[32,16,1408]{2,1,0:T(8,128)(2,1)S(1)}, u32[]{:S(2)}, u32[]{:S(2)}) async-start(bf16[32,16,1408]{2,1,0:T(8,128)(2,1)} %pad_maximum_fusion.2), calls=%async_computation | async-start | bytes 2883584 | tf_op jit(solution)/shard_map/all_to_all | solution.py:628
  19.5 1.0 copy-start.14
  20.5 1.4 copy-start.8
  20.6 2.8 copy-start.15
  23.4 1.4 copy-start.9
  23.4 1.4 copy-start.10
  115.9 3.4 %copy-start.2 = (bf16[32,16,1408]{2,1,0:T(8,128)(2,1)}, bf16[32,16,1408]{2,1,0:T(8,128)(2,1)S(1)}, u32[]{:S(2)}) copy-start(bf16[32,16,1408]{2,1,0:T(8,128)(2,1)S(1)} %all-to-all-done) | copy-start | bytes 4325380
  116.8 2.5 copy-start.13
  116.8 7.7 %slice-start.2 = ((s8[5898240]{0:T(1024)(128)(4,1)}), s8[4194304]{0:T(1024)(128)(4,1)S(1)}, s32[]{:S(2)}) async-start(s8[5898240]{0:T(1024)(128)(4,1)} %bitcast.106), calls=%async_computation.3 | async-start | bytes 8388608
  119.3 5.2 %slice-start.3 = ((s8[5898240]{0:T(1024)(128)(4,1)}), s8[1703936]{0:T(1024)(128)(4,1)S(1)}, s32[]{:S(2)}) async-start(s8[5898240]{0:T(1024)(128)(4,1)} %bitcast.106), calls=%async_computation.4 | async-start | bytes 3407872
  119.3 5.9 %slice-start = ((s8[6291456]{0:T(1024)(128)(4,1)}), s8[4194304]{0:T(1024)(128)(4,1)S(1)}, s32[]{:S(2)}) async-start(s8[6291456]{0:T(1024)(128)(4,1)} %bitcast.101), calls=%async_computation.1 | async-start | bytes 8388608
  121.8 2.7 copy-start.7
  121.8 2.7 copy-start.3
  121.8 3.6 %slice-start.1 = ((s8[6291456]{0:T(1024)(128)(4,1)}), s8[2097152]{0:T(1024)(128)(4,1)S(1)}, s32[]{:S(2)}) async-start(s8[6291456]{0:T(1024)(128)(4,1)} %bitcast.101), calls=%async_computation.2 | async-start | bytes 4194304
  124.5 1.2 copy-start.12
  126.5 2.8 copy-start.5
  129.2 1.1 copy-start.11
  131.2 0.9 copy-start.4
  140.6 6.0 %copy-start.6 = (bf16[256,1280]{1,0:T(8,128)(2,1)S(1)}, bf16[256,1280]{1,0:T(8,128)(2,1)}, u32[]{:S(2)}) copy-start(bf16[256,1280]{1,0:T(8,128)(2,1)} %copy-done.5) | copy-start | bytes 1966084
  295.5 2.5 copy-start.1

commit v3 on v2

--- a/solution.py
+++ b/solution.py
@@ -149,12 +149,6 @@
         else:
             task.copy.wait_recv()
         task.landed = True
-
-
-def take_turns(streams):
-    streams = list(streams)
-    while streams:
-        streams = [stream for stream in streams if next(stream, None) is not None]
 
 
 def cut_y(region, half):
@@ -368,11 +362,24 @@
     return [first.reshape(1280, -1), second.reshape(768, -1), dino, siglip, sam]
 
 
-def reduce_kernel(splits, *refs):
-    count = len(splits)
-    ins, outs = refs[:count], refs[count : 2 * count]
-    sums, last = refs[2 * count : 3 * count], refs[3 * count : 4 * count]
-    spare, (send_sem, recv_sem) = refs[4 * count : -2], refs[-2:]
+WIDTHS = (1536, 1280, 1280)
+FIRST_SPLITS = ((1, 0, 1, 1), (0, 1, 1, 1), (1, 0, 1, 1))
+SECOND_SPLITS = ((0, 2, 2, 2), (2, 0, 1, 2), (0, 2, 2, 1))
+
+
+def adaptor_kernel(factor, *refs):
+    (rows_in, *targets), refs = refs[:4], refs[4:]
+    (first_in, second_in), refs = refs[:2], refs[2:]
+    outs, refs = refs[:6], refs[6:]
+    (first_all, second_all, act, pred, slope), refs = refs[:5], refs[5:]
+    kinds = []
+    for _ in range(8):
+        kinds.append(refs[:3])
+        refs = refs[3:]
+    normed, normed_too, hidden, hidden_too, grad_act, grad_act_too, grad_pred, grad_pred_too = kinds
+    sums, last, refs = refs[:6], refs[6:12], refs[12:]
+    spare, (local_sem, send_sem, recv_sem) = iter(refs[:-3]), refs[-3:]
+    splits = FIRST_SPLITS + SECOND_SPLITS
     at = Place()
     enter(
         [
@@ -386,33 +393,175 @@
         ]
     )
     copies = Copies(send_sem, recv_sem)
-    numbers = itertools.count()
+    tasks = []
+
+    def add_task(*args):
+        tasks.append(Task(*args))
+        return tasks[-1]
+
+    begins = (0, 1536, 2816)
+
+    def fetch(i, src, dst, begin, width, rank):
+        def run():
+            columns = pl.ds(begin, width)
+            copy = pltpu.make_async_copy(src.at[:, columns], dst.at[:, columns], local_sem.at[i])
+            copy.start()
+            return copy
+
+        return add_task("local", src.shape[0] * width, [], run, rank)
+
+    fetched = []
+    for t in range(3):
+        fetched.append(
+            [
+                fetch(2 * t, first_in, first_all, 768 * t, 768, -1),
+                fetch(2 * t + 1, second_in, second_all, begins[t], WIDTHS[t], -1),
+            ]
+        )
+
+    def pick(t):
+        spot = lax.broadcasted_iota(jnp.int32, (256, 512), 0)
+        source = lax.broadcasted_iota(jnp.int32, (256, 512), 1)
+        straight = spot // 8 * 16 + spot % 8
+        flags = jnp.dot(
+            (source == straight).astype(jnp.bfloat16),
+            rows_in[:, 1280:],
+            preferred_element_type=jnp.float32,
+        )
+        shift = jnp.where(flags[:, t : t + 1] > 0.5, 0, 8)
+        normed[t][...] = jnp.dot(
+            (source == straight + shift).astype(jnp.bfloat16),
+            rows_in[:, :1280],
+            preferred_element_type=jnp.float32,
+        ).astype(jnp.bfloat16)
+
+    def forward(t):
+        def run():
+            pick(t)
+            act[...] = jnp.dot(
+                normed[t][...],
+                first_all[:, 768 * t : 768 * t + 768],
+                preferred_element_type=jnp.float32,
+            )
+
+            @pl.loop(0, 16)
+            def _(i):
+                spot = pl.ds(pl.multiple_of(i * 16, 16), 16)
+                hid, tilt = gelu_pair(act[spot, :])
+                hidden[t][spot, :] = hid.astype(jnp.bfloat16)
+                slope[spot, :] = tilt
+
+        return run
+
+    def backward(t):
+        width = WIDTHS[t]
+
+        def run():
+            second = second_all[:, begins[t] : begins[t] + width]
+            pred[:, :width] = jnp.dot(
+                hidden[t][...], second, preferred_element_type=jnp.float32
+            )
+
+            @pl.loop(0, 16)
+            def _(i):
+                spot = pl.ds(pl.multiple_of(i * 16, 16), 16)
+                wanted = targets[t][spot, :].astype(jnp.float32)
+                grad = factor * (pred[spot, :width] - wanted)
+                grad_pred[t][spot, :] = grad.astype(jnp.bfloat16)
+
+            act[...] = lax.dot_general(
+                grad_pred[t][...],
+                second,
+                (((1,), (1,)), ((), ())),
+                preferred_element_type=jnp.float32,
+            )
+
+            @pl.loop(0, 16)
+            def _(i):
+                spot = pl.ds(pl.multiple_of(i * 16, 16), 16)
+                grad_act[t][spot, :] = (act[spot, :] * slope[spot, :]).astype(jnp.bfloat16)
+
+        return run
+
+    def half(width, core):
+        return pl.ds(pl.multiple_of(core * (width // 2), LANE), width // 2)
+
+    def outer(left, right):
+        return lax.dot_general(
+            left, right, (((0,), (0,)), ((), ())), preferred_element_type=jnp.float32
+        )
+
+    def first_grads(t):
+        def run():
+            mine, other = grad_act[t][:, half(768, at.core)], grad_act_too[t][...]
+            for part_of in range(2):
+                columns = slice(640 * part_of, 640 * part_of + 640)
+                total = outer(normed[t][:, columns], mine)
+                total = total + outer(normed_too[t][:, columns], other)
+                sums[t][2 * part_of : 2 * part_of + 2] = total.reshape(2, 4, 2, 40, 384)
+
+        return run
+
+    def second_grads(t):
+        width = WIDTHS[t]
+
+        def run():
+            mine, other = grad_pred[t][:, half(width, at.core)], grad_pred_too[t][...]
+            for part_of in range(2):
+                columns = slice(384 * part_of, 384 * part_of + 384)
+                total = outer(hidden[t][:, columns], mine)
+                total = total + outer(hidden_too[t][:, columns], other)
+                sums[3 + t][2 * part_of : 2 * part_of + 2] = total.reshape(
+                    2, 4, 2, 24, width // 2
+                )
+
+        return run
+
+    def share(src, dst, width, needs, rank):
+        def run():
+            whole = src if width is None else src.at[:, half(width, 1 - at.core)]
+            return copies.send(whole, dst, at.sibling())
+
+        return add_task("sibling", 256 * dst.shape[1] * 2, needs, run, rank)
+
+    ready, before = {}, None
+    for t in range(3):
+        one = add_task("core", 4.0, [fetched[t][0], before], forward(t), 10 * t + 2)
+        got_normed = share(normed[t], normed_too[t], None, [one], t)
+        got_hidden = share(hidden[t], hidden_too[t], None, [one], t)
+        before = add_task("core", 4.0, [fetched[t][1], one], backward(t), 10 * t + 2)
+        got_act = share(grad_act[t], grad_act_too[t], 768, [before], t)
+        got_pred = share(grad_pred[t], grad_pred_too[t], WIDTHS[t], [before], t)
+        ready[t] = add_task("core", 1.5, [before, got_normed, got_act], first_grads(t), 10 * t + 1)
+        ready[3 + t] = add_task(
+            "core", 1.5, [before, got_hidden, got_pred], second_grads(t), 10 * t + 1
+        )
 
     def lanes(k, s):
         return pl.ds(sum(splits[k][:s]) * LANE, splits[k][s] * LANE)
 
-    def wide_lanes(k, s, core):
-        start = core * sum(splits[k]) + sum(splits[k][:s])
-        return pl.ds(pl.multiple_of(start * LANE, LANE), splits[k][s] * LANE)
-
     def view(k, s, region):
         return sums[k].at[part(region[0]), part(region[1]), part(region[2]), :, lanes(k, s)]
 
-    def send(s, region, device, ks=None):
-        sent = []
-        for k in range(count) if ks is None else ks:
-            room = spare[next(numbers)]
-            sent.append((k, room, copies.send(view(k, s, region), room, device)))
-        return sent
-
-    def add(s, sent, region):
-        for k, room, copy in sent:
-            copy.wait_recv()
-            sizes = [extent(entry) for entry in region]
-            steps = [size or 1 for size in sizes]
-
-            @pl.loop(0, steps[0] * steps[1] * steps[2])
-            def _(i, k=k, room=room, sizes=sizes, steps=steps):
+    def send(k, s, region, link, device, needs):
+        room = next(spare)
+
+        def run():
+            return copies.send(view(k, s, region), room, device)
+
+        size = chunks(region) * sums[k].shape[3] * splits[k][s] * LANE * 4
+        task = add_task(link, size, needs, run, k % 3)
+        task.room = room
+        return task
+
+    def add(k, s, region, sent, needs):
+        sizes = [extent(entry) for entry in region]
+        steps = [size or 1 for size in sizes]
+        count = steps[0] * steps[1] * steps[2]
+
+        def run():
+            @pl.loop(0, count)
+            def _(i):
                 spots = (i // (steps[1] * steps[2]), i // steps[2] % steps[1], i % steps[2])
                 there = tuple(spot for spot, size in zip(spots, sizes) if size)
                 here = tuple(
@@ -420,150 +569,143 @@
                     for spot, size, entry in zip(spots, sizes, region)
                 )
                 where = here + (slice(None), lanes(k, s))
-                sums[k][where] = sums[k][where] + room[there + (slice(None), slice(None))]
-
-    def across(s, block):
-        sent = send(s, block(1 - at.z_hi), at.mirror_z())
-        yield True
-        add(s, sent, block(at.z_hi))
-
-    def around(s, block, place, device, cut=None):
-        even, odd = range(0, count, 2), range(1, count, 2)
-        if cut is None:
-            up = send(s, block(place(2)), device(1), even)
-            down = send(s, block(place(2)), device(-1), odd)
+                total = sums[k][where]
+                for task in sent:
+                    total = total + task.room[there + (slice(None), slice(None))]
+                sums[k][where] = total
+
+        size = count * sums[k].shape[3] * splits[k][s] * LANE * 4
+        return add_task("core", 0.1 + size * 0.5e-6, sent + needs, run, -1)
+
+    def across(k, s, needs):
+        sent = send(k, s, (at.y, at.x, 1 - at.z_hi), "mirror", at.mirror_z(), needs)
+        return [add(k, s, (at.y, at.x, at.z_hi), [sent], needs)]
+
+    def across_both(k, s, needs):
+        mine, other = (2 * at.z_lo, 2), (2 - 2 * at.z_lo, 2)
+        sent = send(k, s, (other, ALL, 1 - at.z_hi), "next", at.next_z(), needs)
+        added = add(k, s, (mine, ALL, 1 - at.z_hi), [sent], needs)
+        sent = send(k, s, (mine, ALL, 1 - at.z_hi), "mirror", at.mirror_z(), [added])
+        return [add(k, s, (other, ALL, at.z_hi), [sent], needs)]
+
+    def around(k, s, axis, block, cut, needs):
+        place, device = (at.x_at, at.x_next) if axis == "x" else (at.y_at, at.y_next)
+        here, over, back, ahead = (block(place(step)) for step in (0, 2, -1, 1))
+        up, down = [], []
+        if cut is not None:
+            sent = send(k, s, cut(over, 0), axis + "+", device(1), needs)
+            up.append(add(k, s, cut(ahead, 0), [sent], needs))
+            sent = send(k, s, cut(over, 1), axis + "-", device(-1), needs)
+            down.append(add(k, s, cut(back, 1), [sent], needs))
+        elif k % 2 == 0:
+            sent = send(k, s, over, axis + "+", device(1), needs)
+            up.append(add(k, s, ahead, [sent], needs))
         else:
-            up = send(s, cut(block(place(2)), 0), device(1))
-            down = send(s, cut(block(place(2)), 1), device(-1))
-        yield True
-        add(s, up, block(place(1)) if cut is None else cut(block(place(1)), 0))
-        up = send(s, block(place(1)), device(1))
-        add(s, down, block(place(-1)) if cut is None else cut(block(place(-1)), 1))
-        down = send(s, block(place(-1)), device(-1))
-        yield True
-        add(s, up, block(place(0)))
-        add(s, down, block(place(0)))
-
-    def cut_y(region, half):
-        return ((half * 2, 2), region[1], region[2])
-
-    def cut_x(region, half):
-        return (region[0], (half * 2, 2), region[2])
-
-    def cut_z(region, half):
-        return (region[0], region[1], half)
-
-    chip = [
-        [
-            copies.send(
-                ins[k].at[:, :, :, :, wide_lanes(k, s, 1 - at.core)],
-                sums[k].at[:, :, :, :, lanes(k, s)],
-                at.sibling(),
-            )
-            for k in range(count)
-        ]
-        for s in range(3)
-    ]
-
-    def join(s):
-        for k in range(count):
-            chip[s][k].wait_recv()
-
-            @pl.loop(0, 32)
-            def _(i, k=k):
-                spot = (i // 8, i // 2 % 4, i % 2, slice(None))
-                mine = ins[k][spot + (wide_lanes(k, s, at.core),)]
-                sums[k][spot + (lanes(k, s),)] = sums[k][spot + (lanes(k, s),)] + mine
-
-    def first_stream():
-        join(0)
-        yield from around(0, lambda c: (ALL, c, BOTH), at.x_at, at.x_next, cut_y)
-        yield from around(0, lambda c: (c, at.x, BOTH), at.y_at, at.y_next, cut_z)
-        yield from across(0, lambda c: (at.y, at.x, c))
-
-    def second_stream():
-        join(1)
-        yield from around(1, lambda c: (c, ALL, BOTH), at.y_at, at.y_next, cut_x)
-        yield from across(1, lambda c: (at.y, ALL, c))
-        yield from around(1, lambda c: (at.y, c, at.z_hi), at.x_at, at.x_next)
-
-    def third_stream():
-        join(2)
-        yield from across(2, lambda c: (ALL, ALL, c))
-        yield from around(2, lambda c: (ALL, c, at.z_hi), at.x_at, at.x_next, cut_y)
-        yield from around(2, lambda c: (c, at.x, at.z_hi), at.y_at, at.y_next)
-
-    take_turns([first_stream(), second_stream(), third_stream()])
-    own = (at.y, at.x, at.z_hi)
-    pairs = [copies.send(sums[k].at[own], last[k], at.next_z()) for k in range(count)]
-    halves = []
-    for k in range(count):
-        pairs[k].wait_recv()
-        outs[k][at.core] = sums[k][own] + last[k][...]
-        halves.append(copies.send(outs[k].at[at.core], outs[k].at[at.core], at.sibling()))
-    for copy in halves:
-        copy.wait_recv()
+            sent = send(k, s, over, axis + "-", device(-1), needs)
+            down.append(add(k, s, back, [sent], needs))
+        one = send(k, s, ahead, axis + "+", device(1), needs + up)
+        two = send(k, s, back, axis + "-", device(-1), needs + down)
+        return [add(k, s, here, [one, two], needs)]
+
+    def settle(k, s, needs):
+        own = (at.y, at.x, at.z_hi)
+        where = (slice(None), lanes(k, s))
+
+        def swap():
+            return copies.send(view(k, s, own), last[k].at[:, lanes(k, s)], at.next_z())
+
+        def total():
+            value = sums[k][own + where] + last[k][where]
+            outs[k][(at.core,) + where] = value
+
+        def share_total():
+            place = outs[k].at[at.core, :, lanes(k, s)]
+            return copies.send(place, place, at.sibling())
+
+        size = sums[k].shape[3] * splits[k][s] * LANE * 4
+        swapped = add_task("next", size, needs, swap, -1)
+        added = add_task("core", 0.2, needs + [swapped], total, -1)
+        add_task("sibling", size, [added], share_total, -1)
+
+    for k in range(6):
+        done = [ready[k]]
+        for s in range(4):
+            if splits[k][s] == 0:
+                continue
+            if s == 0:
+                got = around(k, s, "x", lambda c: (ALL, c, BOTH), cut_y, done)
+                got = around(k, s, "y", lambda c: (c, at.x, BOTH), cut_z, got)
+                got = across(k, s, got)
+            elif s == 1:
+                got = around(k, s, "y", lambda c: (c, ALL, BOTH), cut_x, done)
+                got = around(k, s, "x", lambda c: (at.y, c, BOTH), cut_z, got)
+                got = across(k, s, got)
+            elif s == 2:
+                got = across_both(k, s, done)
+                got = around(k, s, "y", lambda c: (c, ALL, at.z_hi), cut_x, got)
+                got = around(k, s, "x", lambda c: (at.y, c, at.z_hi), None, got)
+            else:
+                got = across_both(k, s, done)
+                got = around(k, s, "x", lambda c: (ALL, c, at.z_hi), cut_y, got)
+                got = around(k, s, "y", lambda c: (c, at.x, at.z_hi), None, got)
+            settle(k, s, got)
+    carry_out(plan(tasks))
     copies.finish()
 
 
-def spare_shapes(rows, splits):
-    count = len(rows)
-
-    def room(k, s, lead):
-        return pltpu.VMEM(lead + (rows[k], splits[k][s] * LANE), jnp.float32)
-
-    def across(s, lead):
-        yield [room(k, s, lead) for k in range(count)]
-
-    def around(s, lead, half=None):
-        if half is None:
-            yield [room(k, s, lead) for k in range(0, count, 2)] + [
-                room(k, s, lead) for k in range(1, count, 2)
-            ]
-        else:
-            yield [room(k, s, half) for k in range(count)] * 2
-        yield [room(k, s, lead) for k in range(count)] * 2
-
-    streams = [
-        itertools.chain(around(0, (4, 2), (2, 2)), around(0, (2,), ()), across(0, ())),
-        itertools.chain(around(1, (4, 2), (2, 2)), across(1, (4,)), around(1, ())),
-        itertools.chain(across(2, (4, 4)), around(2, (4,), (2,)), around(2, ())),
-    ]
-    shapes = []
-    while streams:
-        left = []
-        for stream in streams:
-            group = next(stream, None)
-            if group is not None:
-                shapes.extend(group)
-                left.append(stream)
-        streams = left
-    return shapes
-
-
-def reduce_sum(partials, splits):
-    count = len(partials)
-    rows = [p.shape[-2] for p in partials]
-    width = [p.shape[-1] // 2 for p in partials]
+def adaptor_gradients(rows, targets, first_all, second_all, factor):
     inside = pl.BlockSpec(memory_space=pltpu.VMEM)
-    semaphores = pltpu.SemaphoreType.DMA((32 * count,))
-    out = pl.pallas_call(
-        functools.partial(reduce_kernel, splits),
+    whole = pl.BlockSpec(memory_space=pl.ANY)
+    splits = FIRST_SPLITS + SECOND_SPLITS
+    depth = [40] * 3 + [24] * 3
+    width = [384] * 3 + [w // 2 for w in WIDTHS]
+
+    def rooms():
+        plane, line = [(2, 2), (2, 2), (4, 2), (4, 2)], [(), (), (2,), (2,)]
+        column, spot = [(2,), (2,), (4,), (4,)], [(), (), ()]
+        leads = [plane + line + [()]] * 2 + [[(2, 4), (2, 4)] + column + spot] * 2
+        for k in range(6):
+            for s in range(4):
+                if splits[k][s]:
+                    for lead in leads[s]:
+                        yield pltpu.VMEM(lead + (depth[k], splits[k][s] * LANE), jnp.float32)
+
+    def three(*widths):
+        return [pltpu.VMEM((256, w), jnp.bfloat16) for w in widths]
+
+    halves = [w // 2 for w in WIDTHS]
+    semaphores = pltpu.SemaphoreType.DMA((230,))
+    return pl.pallas_call(
+        functools.partial(adaptor_kernel, factor),
         out_shape=[
-            jax.ShapeDtypeStruct((2, r, w), jnp.float32) for r, w in zip(rows, width)
+            jax.ShapeDtypeStruct((2, d, w), jnp.float32) for d, w in zip(depth, width)
         ],
-        in_specs=[inside] * count,
-        out_specs=[inside] * count,
-        scratch_shapes=[pltpu.VMEM((4, 4, 2, r, w), jnp.float32) for r, w in zip(rows, width)]
-        + [pltpu.VMEM((r, w), jnp.float32) for r, w in zip(rows, width)]
-        + spare_shapes(rows, splits)
-        + [semaphores, semaphores],
+        in_specs=[inside] * 4 + [whole] * 2,
+        out_specs=[inside] * 6,
+        scratch_shapes=[
+            pltpu.VMEM(first_all.shape, jnp.bfloat16),
+            pltpu.VMEM(second_all.shape, jnp.bfloat16),
+            pltpu.VMEM((256, 768), jnp.float32),
+            pltpu.VMEM((256, 1536), jnp.float32),
+            pltpu.VMEM((256, 768), jnp.float32),
+            *three(*[1280] * 6),
+            *three(*[768] * 6),
+            *three(*[768] * 3),
+            *three(*[384] * 3),
+            *three(*WIDTHS),
+            *three(*halves),
+            *[pltpu.VMEM((4, 4, 2, d, w), jnp.float32) for d, w in zip(depth, width)],
+            *[pltpu.VMEM((d, w), jnp.float32) for d, w in zip(depth, width)],
+            *rooms(),
+            pltpu.SemaphoreType.DMA((6,)),
+            semaphores,
+            semaphores,
+        ],
         compiler_params=pltpu.CompilerParams(
             collective_id=1, has_side_effects=True, vmem_limit_bytes=62 * 1024 * 1024
         ),
-        name="reduce_gradients",
-    )(*partials)
-    return [jnp.concatenate([o[0], o[1]], axis=-1) for o in out]
+        name="adaptor_gradients",
+    )(rows, *targets, first_all, second_all)
 
 
 def spread(width, group, room):
@@ -574,25 +716,6 @@
 
 def place_columns(values, table):
     return jnp.dot(values, table, preferred_element_type=jnp.float32).astype(jnp.bfloat16)
-
-
-def adaptor_grads(normed, target, first, second, factor):
-    act = jnp.dot(normed, first, preferred_element_type=jnp.float32)
-    hid_full, slope = gelu_pair(act)
-    hidden = hid_full.astype(jnp.bfloat16)
-    pred = jnp.dot(hidden, second, preferred_element_type=jnp.float32)
-    grad_pred = (factor * (pred - target.astype(jnp.float32))).astype(jnp.bfloat16)
-    grad_hid = lax.dot_general(
-        grad_pred, second, (((1,), (1,)), ((), ())), preferred_element_type=jnp.float32
-    )
-    grad_act = (grad_hid * slope).astype(jnp.bfloat16)
-    first_part = lax.dot_general(
-        normed, grad_act, (((0,), (0,)), ((), ())), preferred_element_type=jnp.float32
-    )
-    second_part = lax.dot_general(
-        hidden, grad_pred, (((0,), (0,)), ((), ())), preferred_element_type=jnp.float32
-    )
-    return (first_part, second_part)
 
 
 def student_rows(student_feats, indices):
@@ -632,7 +755,6 @@
         concat_axis=0,
         tiled=True,
     )
-    width = student_feats.shape[-1]
     siglip_room = spread(1152, 36, 40)
     hidden_room = spread(640, 20, 24)
     siglip_turned = jnp.pad(place_columns(siglip_proj.T, siglip_room), ((0, 4), (0, 0)))
@@ -656,41 +778,14 @@
         ],
         ((1, 1, 2, 2), (2, 2, 3, 3), (2, 2, 3, 2), (3, 3, 5, 5)),
     )
-    factor = 2.0 / images_total
-    straight, mirrored = rows[:, :8, :width], rows[:, 8:, :width]
-    first_parts, second_parts = [], []
-    for t, (target, begin, end) in enumerate(
-        zip(targets, (0, 1536, 2816), (1536, 2816, 4096))
-    ):
-        flag = rows[:, :8, width + t : width + t + 1] > 0
-        normed = jnp.where(flag, straight, mirrored).reshape(256, width)
-        one, two = adaptor_grads(
-            normed,
-            target,
-            first_all[:, t * 768 : (t + 1) * 768],
-            second_all[:, begin:end],
-            factor,
-        )
-        first_parts.append(one)
-        second_parts.append(two)
-    first_sum, second_sum = reduce_sum(
-        [
-            jnp.concatenate(first_parts, axis=1).reshape(4, 4, 2, 40, 2304),
-            jnp.concatenate(second_parts, axis=1).reshape(4, 4, 2, 24, 4096),
-        ],
-        ((3, 3, 3), (6, 6, 4)),
+    sums = adaptor_gradients(
+        rows.reshape(512, -1), targets, first_all, second_all, 2.0 / images_total
     )
-    firsts = first_sum.reshape(40, 3, 32, 24)[..., :20].reshape(40, 3, 640)
-    seconds = second_sum[:20]
-    siglip_two = seconds[:, 1536:2816].reshape(20, 32, 40)[..., :36].reshape(20, 1152)
-    return (
-        firsts[:, 0],
-        seconds[:, :1536],
-        firsts[:, 1],
-        siglip_two,
-        firsts[:, 2],
-        seconds[:, 2816:],
-    )
+    joined = [jnp.concatenate([total[0], total[1]], axis=-1) for total in sums]
+    firsts = [total.reshape(40, 32, 24)[..., :20].reshape(40, 640) for total in joined[:3]]
+    seconds = [total[:20] for total in joined[3:]]
+    siglip_two = seconds[1].reshape(20, 32, 40)[..., :36].reshape(20, 1152)
+    return (firsts[0], seconds[0], firsts[1], siglip_two, firsts[2], seconds[2])
 
 
 def solution(mesh):

time: 299 us -> 222 us (0.74)
  matrix products: 39.3 us -> 6.09 us
  other arithmetic: 30.7 us -> 9.48 us
  local copies, waits for them, and re-layouts: 23.6 us -> 10.6 us
  Pallas kernels: 192 us -> 183 us
    dot_general x12 -> x0, matrix products: 33.2 us -> none  [the longest x3 16.8 us: adaptor_grads(): lax.dot_general(normed, grad_act, (((0,), (0,)), ((), ())), preferred_ele...]
    concatenate x3 -> x6, other arithmetic: 20.9 us -> 1.43 us  [body(): joined = [jnp.concatenate([total[0], total[1]], axis=-1) for total in sums]]
    concatenate x2 -> x0, local copies, waits for them, and re-layouts: 13.9 us -> none  [the longest x1 13.6 us: body(): jnp.concatenate(first_parts, axis=1).reshape(4, 4, 2, 40, 2304)]
    pallas_call x1, Pallas kernels: 104 us -> 94.9 us  [adaptor_gradients(): pl.pallas_call(functools.partial(adaptor_kernel, factor), out_shape=[jax....]
  transfers between devices with their start and end apart: 1 -> 1, of which waited for: 0 -> 0; matrix products, arithmetic and copies ran while one was open for 3% -> 4% of each run, Pallas kernels for 30% -> 40%
where the time goes in v3:
time: 222 us; the launch traced here: 221 us
  Pallas kernels  183 us (82%)
  starting transfers between devices  11.3 us (5%)
  local copies, waits for them, and re-layouts  10.6 us (5%)
  other arithmetic  9.48 us (4%)
  matrix products  6.09 us (3%)
    pallas_call x1, Pallas kernels, adaptor_gradients(): pl.pallas_call(functools.partial(adaptor_kernel, factor), out_shape=[jax....  94.9 us
    pallas_call x1, Pallas kernels, gather_and_map(): pl.pallas_call(functools.partial(gather_kernel, splits), out_shape=[jax.S...  87.9 us
    all_to_all x1, starting transfers between devices, body(): lax.all_to_all(student_rows(student_feats, (dino_index, siglip_index, sam...  11.3 us
    dot_general x4, matrix products, place_columns(): jnp.dot(values, table, preferred_element_type=jnp.float32)  6.09 us
  transfers between devices with their start and end apart: 1, of which 0 were waited for; matrix products, arithmetic and copies ran while one was open for 4% of the time, Pallas kernels for 40%

profile of v3, /device:TPU:1, one launch (start us, length us, event | category | flops | bytes accessed | tf_op | source)
XLA Modules:
  0.0 221.3 jit_solution(8599620713491079975)
XLA Ops:
  0.6 0.0 copy-start
  0.6 0.0 copy-start.1
  0.7 0.8 bitcast_compare_fusion.2
  1.4 1.3 convert_reduce_fusion
  2.7 1.4 fusion.7
  4.1 0.7 bitcast_compare_fusion
  4.9 0.1 copy.23
  5.0 0.0 copy-done.1
  5.0 0.3 fusion.8
  5.3 0.1 fusion.44
  5.4 0.6 rev.3
  6.0 1.3 pad_maximum_fusion
  7.3 0.0 copy-start.9
  7.3 0.0 copy-start.10
  7.3 0.0 copy-start.11
  7.3 11.3 %all-to-all-start = ((bf16[32,16,1408]{2,1,0:T(8,128)(2,1)}), bf16[32,16,1408]{2,1,0:T(8,128)(2,1)S(1)}, u32[]{:S(2)}, u32[]{:S(2)}) async-start(bf16[32,16,1408]{2,1,0:T(8,128)(2,1)} %pad_maximum_fusion), calls=%async_computation | async-start | bytes 2883584 | tf_op jit(solution)/shard_map/all_to_all | solution.py:751
  18.7 0.0 copy-done.9
  18.7 0.0 copy-done.10
  18.7 0.0 copy-done.11
  18.8 0.0 copy-start.7
  18.8 0.8 fusion.9
  19.6 0.0 copy-done.7
  19.6 0.0 copy-start.4
  19.7 0.0 copy-start.8
  19.7 1.4 fusion.1
  21.1 0.0 copy-done.4
  21.1 0.7 fusion.22.refs_1_
  21.8 0.7 pad_maximum_fusion.5.refs_2_
  22.5 0.0 copy-done.8
  22.5 0.0 copy-start.5
  22.5 0.0 copy-start.6
  22.5 1.3 fusion.2
  23.8 0.0 copy-done.5
  23.8 0.0 copy-done.6
  23.8 0.7 fusion.24.refs_3_
  24.5 0.0 copy-done
  24.5 2.5 %fusion.refs_5_ = bf16[256,1280]{1,0:T(8,128)(2,1)} fusion(bf16[32,8,1152]{2,1,0:T(8,128)(2,1)S(1)} %copy-done, s32[1152]{0:T(1024)S(1)} %get-tuple-element.54, s32[1152]{0:T(1024)S(1)} %get-tuple-element.55, s32[1152]{0:T(1024)S(1)} %get-tuple-element.53, s32[1152]{0:T(1024)S(1)} %get-tuple-element.56, pred[1152]{0:T(1024)(128)(4,1)S(1)} %get-tuple-element.57, ...), kind=kOutput, calls=%fused_computation.2 | convolution fusion | flops 762675200 | bytes 1265920 | tf_op jit(solution)/shard_map/dot_general | solution.py:718
  27.1 87.9 %gather_and_map.1 = (bf16[4,4,2,40,2304]{4,3,2,1,0:T(8,128)(2,1)}, bf16[4,4,2,24,4096]{4,3,2,1,0:T(8,128)(2,1)}, bf16[256,1536]{1,0:T(8,128)(2,1)}, bf16[256,1280]{1,0:T(8,128)(2,1)}, bf16[256,1280]{1,0:T(8,128)(2,1)}) custom-call(bf16[48,1536]{1,0:T(8,128)(2,1)} %bitcast.79, bf16[40,2560]{1,0:T(8,128)(2,1)} %fusion.22.refs_1_, ...), custom_call_target="tpu_custom_call" | custom-call | tf_op jit(solution)/shard_map/gather_and_map/pallas_call | solution.py:337
  115.0 0.0 all-to-all-done
  115.0 0.0 copy-start.2
  115.0 1.2 copy-done.2
  116.2 94.9 %adaptor_gradients.1 = (f32[2,40,384]{2,1,0:T(8,128)}, f32[2,40,384]{2,1,0:T(8,128)}, f32[2,40,384]{2,1,0:T(8,128)}, f32[2,24,768]{2,1,0:T(8,128)}, f32[2,24,640]{2,1,0:T(8,128)}, /*index=5*/f32[2,24,640]{2,1,0:T(8,128)}) custom-call(bf16[512,1408]{1,0:T(8,128)(2,1)} %bitcast.67, bf16[256,1536]{1,0:T(8,128)(2,1)} %get-tuple-element.17.refs_1_, ...), custom_call_target="tpu_custom_call" | custom-call | tf_op jit(solution)/shard_map/adaptor_gradients/pallas_call | solution.py:678
  211.0 0.0 copy-start.3
  211.1 0.9 fusion.48
  212.0 0.9 fusion.47
  212.8 0.9 slice_bitcast_fusion.5
  213.7 0.9 fusion.46
  214.6 0.9 slice_bitcast_fusion.3
  215.4 0.1 copy.29
  215.6 0.1 copy.27
  215.7 0.1 copy.25
  215.8 0.0 copy-done.3
  215.9 0.1 copy.30
  216.1 0.8 copy.33
  216.9 0.1 copy.28
  217.1 0.8 copy.32
  217.9 0.1 copy.26
  218.1 0.8 copy.31
  218.9 0.2 reshape.138
  219.1 0.9 reshape.139
  220.0 0.7 pad_maximum_fusion.7
  220.6 0.7 pad_maximum_fusion.6
  (19 shorter events, 0.3 us)
Async XLA Ops:
  0.6 23.9 %copy-start = (bf16[32,8,1152]{2,1,0:T(8,128)(2,1)S(1)}, bf16[32,8,1152]{2,1,0:T(8,128)(2,1)}, u32[]{:S(2)}) copy-start(bf16[32,8,1152]{2,1,0:T(8,128)(2,1)} %param.18) | copy-start | bytes 1769476
  0.6 4.3 %copy-start.1 = (bf16[1,256,1280]{2,1,0:T(8,128)(2,1)S(1)}, bf16[1,256,1280]{2,1,0:T(8,128)(2,1)}, u32[]{:S(2)}) copy-start(bf16[1,256,1280]{2,1,0:T(8,128)(2,1)} %param.16) | copy-start | bytes 1966084
  7.3 11.4 %copy-start.9 = (bf16[40,640]{1,0:T(8,128)(2,1)S(1)}, bf16[40,640]{1,0:T(8,128)(2,1)}, u32[]{:S(2)}) copy-start(bf16[40,640]{1,0:T(8,128)(2,1)} %param.30) | copy-start | bytes 153604
  7.3 11.4 %copy-start.10 = (bf16[40,640]{1,0:T(8,128)(2,1)S(1)}, bf16[40,640]{1,0:T(8,128)(2,1)}, u32[]{:S(2)}) copy-start(bf16[40,640]{1,0:T(8,128)(2,1)} %param.28) | copy-start | bytes 153604
  7.3 11.4 %copy-start.11 = (bf16[40,640]{1,0:T(8,128)(2,1)S(1)}, bf16[40,640]{1,0:T(8,128)(2,1)}, u32[]{:S(2)}) copy-start(bf16[40,640]{1,0:T(8,128)(2,1)} %param.26) | copy-start | bytes 153604
  7.3 107.7 %all-to-all-start = ((bf16[32,16,1408]{2,1,0:T(8,128)(2,1)}), bf16[32,16,1408]{2,1,0:T(8,128)(2,1)S(1)}, u32[]{:S(2)}, u32[]{:S(2)}) async-start(bf16[32,16,1408]{2,1,0:T(8,128)(2,1)} %pad_maximum_fusion), calls=%async_computation | async-start | bytes 2883584 | tf_op jit(solution)/shard_map/all_to_all | solution.py:751
  18.8 0.9 copy-start.7
  19.6 1.4 copy-start.4
  19.7 2.8 %copy-start.8 = (bf16[20,1152]{1,0:T(8,128)(2,1)S(1)}, bf16[20,1152]{1,0:T(8,128)(2,1)}, u32[]{:S(2)}) copy-start(bf16[20,1152]{1,0:T(8,128)(2,1)} %param.29) | copy-start | bytes 138244
  22.5 1.4 copy-start.5
  22.5 1.4 copy-start.6
  115.0 1.2 copy-start.2
  211.0 4.8 %copy-start.3 = (f32[2,24,768]{2,1,0:T(8,128)S(1)}, f32[2,24,768]{2,1,0:T(8,128)}, u32[]{:S(2)}) copy-start(f32[2,24,768]{2,1,0:T(8,128)} %get-tuple-element.23) | copy-start | bytes 442372
